TPU v7x, 32 devices: a whole 2x2x4 slice. The times are simulated.
32 devices in a mesh: wide: 8 (over z, x), narrow: 4 (over y, core).
Axes of the slice: x: 2, y: 2, z: 4, core: 2. Of those that a mesh axis runs over, the one named last changes fastest.
Arguments:
- tokens: bfloat16 [64, 1024, 480], P(('wide', 'narrow')), may hold values from -6 to 6
- segment_ids: int32 [64, 1024], P(('wide', 'narrow')), may hold values from 0 to 3, never falling along the last dimension, each value on 1 to 512 neighbouring positions
- pad_mask: int32 [64, 1024], P(('wide', 'narrow')), may hold values 0 or 1
- cotangent: bfloat16 [64, 1024, 480], P(('wide', 'narrow')), may hold values from -6 to 6
- qkv_weight: float32 [691200], P(('wide', 'narrow')), may hold values from -0.25 to 0.25
- qkv_first: float32 [691200], P(('wide', 'narrow')), may hold values from -256 to 256
- qkv_second: float32 [691200], P(('wide', 'narrow')), may hold values from 65536 to 262144
- out_weight: float32 [230400], P(('wide', 'narrow')), may hold values from -6 to 6
- out_first: float32 [230400], P(('wide', 'narrow')), may hold values from -22.627417 to 22.627417
- out_second: float32 [230400], P(('wide', 'narrow')), may hold values from 512 to 2048
- up_weight: float32 [921600], P(('wide', 'narrow')), may hold values from -0.25 to 0.25
- up_first: float32 [921600], P(('wide', 'narrow')), may hold values from -89.6 to 89.6
- up_second: float32 [921600], P(('wide', 'narrow')), may hold values from 7864.32 to 31457.28
- down_weight: float32 [921600], P(('wide', 'narrow')), may hold values from -0.125 to 0.125
- down_first: float32 [921600], P(('wide', 'narrow')), may hold values from -204.8 to 204.8
- down_second: float32 [921600], P(('wide', 'narrow')), may hold values from 41943.04 to 167772.16
- gains: float32 [960], replicated, may hold values from 0.5 to 1.5
- gain_first: float32 [960], replicated, may hold values from -256 to 256
- gain_second: float32 [960], replicated, may hold values from 65536 to 262144
- biases: float32 [5280], replicated, may hold values from -1.75 to 1.75
- bias_first: float32 [5280], replicated, may hold values from -256 to 256
- bias_second: float32 [5280], replicated, may hold values from 65536 to 262144
Outputs:
- outputs: bfloat16 [64, 1024, 480], P(('wide', 'narrow'))
- input_grad: float32 [64, 1024, 480], P(('wide', 'narrow'))
- qkv_grad: float32 [691200], P(('wide', 'narrow'))
- qkv_new: float32 [691200], P(('wide', 'narrow'))
- qkv_first_new: float32 [691200], P(('wide', 'narrow'))
- qkv_second_new: float32 [691200], P(('wide', 'narrow'))
- out_grad: float32 [230400], P(('wide', 'narrow'))
- out_new: float32 [230400], P(('wide', 'narrow'))
- out_first_new: float32 [230400], P(('wide', 'narrow'))
- out_second_new: float32 [230400], P(('wide', 'narrow'))
- up_grad: float32 [921600], P(('wide', 'narrow'))
- up_new: float32 [921600], P(('wide', 'narrow'))
- up_first_new: float32 [921600], P(('wide', 'narrow'))
- up_second_new: float32 [921600], P(('wide', 'narrow'))
- down_grad: float32 [921600], P(('wide', 'narrow'))
- down_new: float32 [921600], P(('wide', 'narrow'))
- down_first_new: float32 [921600], P(('wide', 'narrow'))
- down_second_new: float32 [921600], P(('wide', 'narrow'))
- gain_grad: float32 [960], replicated
- gain_new: float32 [960], replicated
- gain_first_new: float32 [960], replicated
- gain_second_new: float32 [960], replicated
- bias_grad: float32 [5280], replicated
- bias_new: float32 [5280], replicated
- bias_first_new: float32 [5280], replicated
- bias_second_new: float32 [5280], replicated
- down_bias_grad: float32 [480], replicated
Inputs may be any that keep to these rules, and one draw needn't show every extreme that they name: `segment_ids`: within a row the ids never fall; each of the 4 proteins of a row holds 1 to 512 residues, and some protein holds 512.
All inputs are finite; a program needn't handle non-finite values. No bound on the sum of `pad_mask` on one device may be relied on, other than what follows from the above.
Results may differ from a plain program's by a relative error of at most 0.012.
Values may be sent and summed in bfloat16 or wider, within the bound.
No kernel may reach another device: no remote copies, remote signals or barrier semaphores. Data moves between devices by JAX's collectives and lax.ppermute only.
A program may use at most 192 MiB of HBM per device.

v0:
```python
import functools
import math

import jax
import jax.numpy as jnp
from jax import lax
from jax.sharding import PartitionSpec as P

D = 480
HEAD_DIM = 24
FF = 1920
STEP = 3


def layer_norm(field, gain_row, offset):
    average = jnp.mean(field, axis=-1, keepdims=True)
    centered = field - average
    spread = jnp.mean(centered * centered, axis=-1, keepdims=True)
    return centered * lax.rsqrt(spread + 1e-05) * gain_row + offset


def positions_of(segments):
    places = lax.broadcasted_iota(jnp.int32, segments.shape, segments.ndim - 1)
    change = jnp.concatenate(
        [
            jnp.ones(segments.shape[:-1] + (1,), dtype=jnp.bool_),
            segments[..., 1:] != segments[..., :-1],
        ],
        axis=-1,
    )
    starts = lax.cummax(jnp.where(change, places, 0), axis=segments.ndim - 1)
    return (places - starts).astype(jnp.float32)


def angles(segments):
    half_dim = HEAD_DIM // 2
    frequency = jnp.exp(jnp.arange(half_dim).astype(jnp.float32) * (-math.log(10000.0) / half_dim))
    phases = positions_of(segments)[..., None] * frequency
    return (jnp.cos(phases)[..., None, :], jnp.sin(phases)[..., None, :])


def rotate(field, cosine, sine_part):
    half_dim = field.shape[-1] // 2
    front_half = field[..., :half_dim]
    back_half = field[..., half_dim:]
    return jnp.concatenate(
        [front_half * cosine - back_half * sine_part, back_half * cosine + front_half * sine_part],
        axis=-1,
    )


def allowed_mask(segments, pad_mask):
    length = segments.shape[-1]
    diagonal = jnp.arange(length)[:, None] == jnp.arange(length)[None, :]
    return (segments[:, :, None] == segments[:, None, :]) & (
        (pad_mask[:, None, :] == 1) | diagonal[None]
    )


def masked_scores(queries, keys_low, allowed):
    scores = jnp.einsum("rie,rje->rij", queries, keys_low, preferred_element_type=jnp.float32)
    return jnp.where(allowed, scores, -1e30)


def head_forward(triple, allowed):
    scores = masked_scores(triple[0], triple[1], allowed)
    highest = jnp.max(scores, axis=-1, keepdims=True)
    weighted = jnp.exp(scores - highest)
    totals = jnp.sum(weighted, axis=-1, keepdims=True)
    attn_probs = weighted / totals
    attended = jnp.einsum(
        "rij,rje->rie",
        attn_probs.astype(jnp.bfloat16),
        triple[2],
        preferred_element_type=jnp.float32,
    )
    return (attended, (highest + jnp.log(totals))[..., 0])


def head_backward(packed, allowed):
    queries, keys_low, values, grad_heads, log_totals = packed
    scores = masked_scores(queries, keys_low, allowed)
    attn_probs = jnp.exp(scores - log_totals[..., None])
    grad_probs = jnp.einsum("rie,rje->rij", grad_heads, values, preferred_element_type=jnp.float32)
    delta_rows = jnp.sum(attn_probs * grad_probs, axis=-1, keepdims=True)
    grad_scores = (attn_probs * (grad_probs - delta_rows)).astype(jnp.bfloat16)
    grad_queries = jnp.einsum(
        "rij,rje->rie", grad_scores, keys_low, preferred_element_type=jnp.float32
    )
    grad_keys = jnp.einsum("rij,rie->rje", grad_scores, queries, preferred_element_type=jnp.float32)
    grad_values = jnp.einsum(
        "rij,rie->rje",
        attn_probs.astype(jnp.bfloat16),
        grad_heads,
        preferred_element_type=jnp.float32,
    )
    return (grad_queries, grad_keys, grad_values)


def adamw_update(weight, first, second, gradient, learn_rate, step_value):
    first_new = 0.5 * first + 0.5 * gradient
    second_new = 0.5 * second + 0.5 * gradient * gradient
    correction = 1.0 - 0.5**step_value
    stepped = first_new / correction / (jnp.sqrt(second_new / correction) + 1e-08)
    return (weight - learn_rate * (stepped + 0.01 * weight), first_new, second_new)


def shards(
    tokens,
    segment_ids,
    pad_mask,
    cotangent,
    qkv_weight,
    qkv_first,
    qkv_second,
    out_weight,
    out_first,
    out_second,
    up_weight,
    up_first,
    up_second,
    down_weight,
    down_first,
    down_second,
    gains,
    gain_first,
    gain_second,
    biases,
    bias_first,
    bias_second,
):
    row_count, length, model_width = tokens.shape
    head_count = model_width // HEAD_DIM
    token_count = row_count * length
    fetched = (
        lax.all_gather(qkv_weight.astype(jnp.bfloat16), ("wide", "narrow"), axis=0, tiled=True),
        lax.all_gather(out_weight.astype(jnp.bfloat16), ("wide", "narrow"), axis=0, tiled=True),
        lax.all_gather(up_weight.astype(jnp.bfloat16), ("wide", "narrow"), axis=0, tiled=True),
        lax.all_gather(down_weight.astype(jnp.bfloat16), ("wide", "narrow"), axis=0, tiled=True),
    )
    w_qkv = fetched[0].reshape(D, 3 * D)
    w_out = fetched[1].reshape(D, D)
    w_up = fetched[2].reshape(D, FF)
    w_down = fetched[3].reshape(FF, D)
    cosine, sine_part = angles(segment_ids)
    allowed = allowed_mask(segment_ids, pad_mask)
    query_scale = HEAD_DIM ** (-0.5)

    def turn_query(part):
        return rotate(part, cosine, sine_part) * query_scale

    def turn_key(part):
        return rotate(part, cosine, sine_part)

    flat_tokens = tokens.reshape(token_count, D).astype(jnp.float32)
    normed = layer_norm(flat_tokens, gains[:D], biases[:D])
    normed_low = normed.astype(jnp.bfloat16)
    mixed_qkv = jnp.dot(normed_low, w_qkv, preferred_element_type=jnp.float32) + biases[D : 4 * D]
    split_qkv = mixed_qkv.reshape(row_count, length, 3, head_count, HEAD_DIM)
    queries = turn_query(split_qkv[:, :, 0]).astype(jnp.bfloat16)
    keys_low = turn_key(split_qkv[:, :, 1]).astype(jnp.bfloat16)
    values = split_qkv[:, :, 2].astype(jnp.bfloat16)
    head_queries = jnp.moveaxis(queries, 2, 0)
    head_keys = jnp.moveaxis(keys_low, 2, 0)
    head_values = jnp.moveaxis(values, 2, 0)
    attended_heads, log_totals = lax.map(
        functools.partial(head_forward, allowed=allowed), (head_queries, head_keys, head_values)
    )
    attended = jnp.moveaxis(attended_heads, 0, 2).reshape(token_count, D).astype(jnp.bfloat16)
    branch = jnp.dot(attended, w_out, preferred_element_type=jnp.float32) + biases[4 * D : 5 * D]
    middle = flat_tokens + branch
    normed_two = layer_norm(middle, gains[D:], biases[5 * D : 6 * D])
    normed_two_low = normed_two.astype(jnp.bfloat16)
    hidden = (
        jnp.dot(normed_two_low, w_up, preferred_element_type=jnp.float32)
        + biases[6 * D : 6 * D + FF]
    )
    active = jax.nn.gelu(hidden, approximate=False).astype(jnp.bfloat16)
    result_rows = (
        middle + jnp.dot(active, w_down, preferred_element_type=jnp.float32) + biases[6 * D + FF :]
    )
    outputs = result_rows.astype(jnp.bfloat16).reshape(tokens.shape)
    regathered = (
        lax.all_gather(qkv_weight.astype(jnp.bfloat16), ("wide", "narrow"), axis=0, tiled=True),
        lax.all_gather(out_weight.astype(jnp.bfloat16), ("wide", "narrow"), axis=0, tiled=True),
        lax.all_gather(up_weight.astype(jnp.bfloat16), ("wide", "narrow"), axis=0, tiled=True),
        lax.all_gather(down_weight.astype(jnp.bfloat16), ("wide", "narrow"), axis=0, tiled=True),
    )
    back_qkv = regathered[0].reshape(D, 3 * D)
    back_out = regathered[1].reshape(D, D)
    back_up = regathered[2].reshape(D, FF)
    back_down = regathered[3].reshape(FF, D)
    grad_rows = cotangent.reshape(token_count, D).astype(jnp.float32)
    grad_two = grad_rows.astype(jnp.bfloat16)
    down_term = jnp.einsum("nf,nd->fd", active, grad_two, preferred_element_type=jnp.float32)
    down_bias = jnp.sum(grad_two.astype(jnp.float32), axis=0)
    grad_active = jnp.einsum("nd,fd->nf", grad_two, back_down, preferred_element_type=jnp.float32)
    gelu_value, gelu_back = jax.vjp(functools.partial(jax.nn.gelu, approximate=False), hidden)
    grad_hidden = gelu_back(grad_active)[0].astype(jnp.bfloat16)
    up_term = jnp.einsum(
        "nd,nf->df", normed_two_low, grad_hidden, preferred_element_type=jnp.float32
    )
    up_bias = jnp.sum(grad_hidden.astype(jnp.float32), axis=0)
    grad_normed_two = jnp.einsum(
        "nf,df->nd", grad_hidden, back_up, preferred_element_type=jnp.float32
    )
    norm_value, second_back = jax.vjp(layer_norm, middle, gains[D:], biases[5 * D : 6 * D])
    grad_middle_part, gain_two_grad, shift_two_grad = second_back(grad_normed_two)
    grad_middle = grad_rows + grad_middle_part
    grad_branch = grad_middle.astype(jnp.bfloat16)
    out_term = jnp.einsum("ni,nd->id", attended, grad_branch, preferred_element_type=jnp.float32)
    out_bias = jnp.sum(grad_branch.astype(jnp.float32), axis=0)
    grad_attended = jnp.einsum(
        "nd,id->ni", grad_branch, back_out, preferred_element_type=jnp.float32
    ).astype(jnp.bfloat16)
    grad_heads = jnp.moveaxis(grad_attended.reshape(row_count, length, head_count, HEAD_DIM), 2, 0)
    grad_queries, grad_keys, grad_values = lax.map(
        functools.partial(head_backward, allowed=allowed),
        (head_queries, head_keys, head_values, grad_heads, log_totals),
    )
    query_value, query_back = jax.vjp(turn_query, split_qkv[:, :, 0])
    key_value, key_back = jax.vjp(turn_key, split_qkv[:, :, 1])
    grad_query_pre = query_back(jnp.moveaxis(grad_queries, 0, 2))[0]
    grad_key_pre = key_back(jnp.moveaxis(grad_keys, 0, 2))[0]
    grad_mixed = jnp.stack([grad_query_pre, grad_key_pre, jnp.moveaxis(grad_values, 0, 2)], axis=2)
    grad_mixed = grad_mixed.reshape(token_count, 3 * D).astype(jnp.bfloat16)
    qkv_term = jnp.einsum("nd,nc->dc", normed_low, grad_mixed, preferred_element_type=jnp.float32)
    qkv_bias = jnp.sum(grad_mixed.astype(jnp.float32), axis=0)
    grad_normed = jnp.einsum("nc,dc->nd", grad_mixed, back_qkv, preferred_element_type=jnp.float32)
    first_value, first_back = jax.vjp(layer_norm, flat_tokens, gains[:D], biases[:D])
    grad_flat, gain_one_grad, shift_one_grad = first_back(grad_normed)
    input_grad = (grad_middle + grad_flat).reshape(tokens.shape)
    qkv_grad, out_grad, up_grad, down_grad = (
        lax.psum_scatter(qkv_term.reshape(-1), ("wide", "narrow"), scatter_dimension=0, tiled=True),
        lax.psum_scatter(out_term.reshape(-1), ("wide", "narrow"), scatter_dimension=0, tiled=True),
        lax.psum_scatter(up_term.reshape(-1), ("wide", "narrow"), scatter_dimension=0, tiled=True),
        lax.psum_scatter(
            down_term.reshape(-1), ("wide", "narrow"), scatter_dimension=0, tiled=True
        ),
    )
    gain_local = jnp.concatenate([gain_one_grad, gain_two_grad])
    bias_local = jnp.concatenate(
        [shift_one_grad, qkv_bias, out_bias, shift_two_grad, up_bias, down_bias]
    )
    gain_grad, bias_grad = lax.psum((gain_local, bias_local), ("wide", "narrow"))
    down_bias_grad = bias_grad[6 * D + FF :]
    step_value = float(STEP)
    qkv_new, qkv_first_new, qkv_second_new = adamw_update(
        qkv_weight, qkv_first, qkv_second, qkv_grad, 0.05, step_value
    )
    out_new, out_first_new, out_second_new = adamw_update(
        out_weight, out_first, out_second, out_grad, 0.3, step_value
    )
    up_new, up_first_new, up_second_new = adamw_update(
        up_weight, up_first, up_second, up_grad, 0.05, step_value
    )
    down_new, down_first_new, down_second_new = adamw_update(
        down_weight, down_first, down_second, down_grad, 0.03, step_value
    )
    gain_new, gain_first_new, gain_second_new = adamw_update(
        gains, gain_first, gain_second, gain_grad, 0.2, step_value
    )
    bias_new, bias_first_new, bias_second_new = adamw_update(
        biases, bias_first, bias_second, bias_grad, 0.1, step_value
    )
    return (
        outputs,
        input_grad,
        qkv_grad,
        qkv_new,
        qkv_first_new,
        qkv_second_new,
        out_grad,
        out_new,
        out_first_new,
        out_second_new,
        up_grad,
        up_new,
        up_first_new,
        up_second_new,
        down_grad,
        down_new,
        down_first_new,
        down_second_new,
        gain_grad,
        gain_new,
        gain_first_new,
        gain_second_new,
        bias_grad,
        bias_new,
        bias_first_new,
        bias_second_new,
        down_bias_grad,
    )


def solution(mesh):
    in_specs = (
        P(("wide", "narrow"), None, None),
        P(("wide", "narrow"), None),
        P(("wide", "narrow"), None),
        P(("wide", "narrow"), None, None),
        P(("wide", "narrow")),
        P(("wide", "narrow")),
        P(("wide", "narrow")),
        P(("wide", "narrow")),
        P(("wide", "narrow")),
        P(("wide", "narrow")),
        P(("wide", "narrow")),
        P(("wide", "narrow")),
        P(("wide", "narrow")),
        P(("wide", "narrow")),
        P(("wide", "narrow")),
        P(("wide", "narrow")),
        P(),
        P(),
        P(),
        P(),
        P(),
        P(),
    )
    out_specs = (
        P(("wide", "narrow"), None, None),
        P(("wide", "narrow"), None, None),
        P(("wide", "narrow")),
        P(("wide", "narrow")),
        P(("wide", "narrow")),
        P(("wide", "narrow")),
        P(("wide", "narrow")),
        P(("wide", "narrow")),
        P(("wide", "narrow")),
        P(("wide", "narrow")),
        P(("wide", "narrow")),
        P(("wide", "narrow")),
        P(("wide", "narrow")),
        P(("wide", "narrow")),
        P(("wide", "narrow")),
        P(("wide", "narrow")),
        P(("wide", "narrow")),
        P(("wide", "narrow")),
        P(),
        P(),
        P(),
        P(),
        P(),
        P(),
        P(),
        P(),
        P(),
    )
    return jax.shard_map(shards, mesh=mesh, in_specs=in_specs, out_specs=out_specs, check_vma=False)
```

profile of v0, /device:TPU:0, one launch (start us, length us, event | category | flops | bytes accessed | tf_op | source)
XLA Modules:
  0.0 1512.2 jit_solution(1676026667574397939)
XLA Ops:
  20.7 4.8 copy.104
  33.6 115.3 %all-reduce.19.cloned.1.call-done = (bf16[691200]{0:T(1024)(128)(2,1)}, bf16[230400]{0:T(1024)(128)(2,1)}) async-done(((bf16[691200]{0:T(1024)(128)(2,1)}, bf16[230400]{0:T(1024)(128)(2,1)}), (bf16[691200]{0:T(1024)(128)(2,1)}, bf16[230400]{0:T(1024)(128)(2,1)})) %all-reduce.19.cloned.1.call-update) | async-done | bytes 1843216
  152.3 8.3 convolution_add_fusion
  160.7 16.3 %reshape.320 = f32[2,1024,3,20,24]{1,0,4,3,2:T(2,128)} reshape(f32[2048,1440]{0,1:T(8,128)} %convolution_add_fusion) | data formatting | bytes 23592960 | tf_op jit(solution)/shard_map/reshape | solution.py:159
  177.0 8.5 fusion.96
  200.7 237.9 %while.30 = (s32[]{:T(128)}, bf16[20,2,1024,24]{2,3,1,0:T(8,128)(2,1)S(1)}, f32[20,2,1024]{2,1,0:T(2,128)}, bf16[20,2,1024,24]{2,3,1,0:T(8,128)(2,1)}, bf16[20,2...) while((s32[]{:T(128)}, ...), condition=%wide.region_7.8_spmd.clone.clone, body=%wide.region_4.7_spmd.clone.sunk.clone | while | flops 239073280 | bytes 28921960 | solution.py:166
  449.2 39.5 %reduce.5 = bf16[32,28800]{1,0:T(8,128)(2,1)S(1)} reduce(bf16[32,1,28800]{2,1,0:T(2,128)(2,1)} %all-gather.5.cloned.1.call-done, bf16[]{:T(256)} %constant.210), dimensions={1}, to_apply=%all-gather.reduce_sub_computation | reduce | bytes 3686402 | tf_op jit(solution)/shard_map/all_gather | solution.py:138
  492.4 39.9 %reduce.6 = bf16[32,28800]{1,0:T(8,128)(2,1)S(1)} reduce(bf16[32,1,28800]{2,1,0:T(2,128)(2,1)} %all-gather.7.cloned.1.call-done, bf16[]{:T(256)} %constant.210), dimensions={1}, to_apply=%all-gather.1.reduce_sub_computation | reduce | bytes 3686402 | tf_op jit(solution)/shard_map/all_gather | solution.py:139
  536.2 44.0 %multiply_convert_fusion.1 = (bf16[2048,1920]{1,0:T(8,128)(2,1)}, f32[2048,1920]{1,0:T(8,128)}, f32[2048,1920]{1,0:T(8,128)}) fusion(f32[1920]{0:T(1024)S(1)} %copy-done.65, bf16[480,1920]{1,0:T(8,128)(2,1)} %reshape.324, f32[2048,480]{0,1:T(8,128)} %copy-done.2, f32[480]{0:T(512)S(1)} %copy-done.73, f32[480]{0:T(512)S(1)} %get-tuple-element.376, ...), kind=kOutput, calls=%fused_computation.57 | convolution fusion | flops 4039311360 | bytes 45124864 | tf_op jit(solution)/shard_map/dot_general | solution.py:175
  580.3 17.7 %convert_reduce_fusion = (f32[1920]{0:T(1024)}, bf16[2048,1920]{1,0:T(8,128)(2,1)}) fusion(f32[2048,1920]{1,0:T(8,128)} %get-tuple-element.343, bf16[2048,480]{0,1:T(8,128)(2,1)S(1)} %bitcast.229, bf16[1920,480]{1,0:T(8,128)(2,1)} %reshape.325, f32[2048,1920]{1,0:T(8,128)} %get-tuple-element.380, f32[1920]{0:T(1024)S(1)} %copy-done.65), kind=kOutput, calls=%fused_computation.55 | convolution fusion | flops 3841718272 | bytes 43146240 | tf_op jit(solution)/shard_map/nd,fd->nf/dot_general | solution.py:197
  598.0 10.4 multiply_reduce_fusion.1
  616.6 6.2 fusion.84
  622.8 6.1 reshape.328
  632.3 585.6 %while.31 = (s32[]{:T(128)}, f32[20,2,1024,24]{2,3,1,0:T(8,128)}, f32[20,2,1024,24]{2,3,1,0:T(8,128)}, bf16[20,2,1024,24]{2,3,1,0:T(8,128)(2,1)}, bf16[20,2,1024...) while((s32[]{:T(128)}, f32[20,2,1024,24]{2,3,1,0:T(8,128)}, ...), condition=%wide.region_14.15_spmd.clone.clone, body=%wide.region_12.14_spmd.clone.sunk.clone | while | flops 526383104 | bytes 114590928 | solution.py:217
  635.3 7.1 multiply_reduce_fusion.8
  642.4 8.1 multiply_convert_fusion.4
  664.5 7.1 multiply_reduce_fusion.8
  671.7 8.1 multiply_convert_fusion.4
  684.9 4.6 fusion.175
  693.8 7.1 multiply_reduce_fusion.8
  700.9 8.1 multiply_convert_fusion.4
  723.0 7.1 multiply_reduce_fusion.8
  730.2 8.1 multiply_convert_fusion.4
  752.3 7.1 multiply_reduce_fusion.8
  759.4 8.1 multiply_convert_fusion.4
  781.5 7.1 multiply_reduce_fusion.8
  788.7 8.1 multiply_convert_fusion.4
  810.8 7.1 multiply_reduce_fusion.8
  818.0 8.1 multiply_convert_fusion.4
  840.1 7.1 multiply_reduce_fusion.8
  847.2 8.1 multiply_convert_fusion.4
  869.4 7.1 multiply_reduce_fusion.8
  876.5 8.1 multiply_convert_fusion.4
  898.6 7.1 multiply_reduce_fusion.8
  905.7 8.1 multiply_convert_fusion.4
  927.9 7.1 multiply_reduce_fusion.8
  935.0 8.1 multiply_convert_fusion.4
  957.1 7.1 multiply_reduce_fusion.8
  964.3 8.1 multiply_convert_fusion.4
  986.4 7.1 multiply_reduce_fusion.8
  993.6 8.1 multiply_convert_fusion.4
  1015.7 7.1 multiply_reduce_fusion.8
  1022.8 8.1 multiply_convert_fusion.4
  1045.0 7.1 multiply_reduce_fusion.8
  1052.1 8.1 multiply_convert_fusion.4
  1074.2 7.1 multiply_reduce_fusion.8
  1081.3 8.1 multiply_convert_fusion.4
  1103.5 7.1 multiply_reduce_fusion.8
  1110.6 8.1 multiply_convert_fusion.4
  1132.7 7.1 multiply_reduce_fusion.8
  1139.8 8.1 multiply_convert_fusion.4
  1162.0 7.1 multiply_reduce_fusion.8
  1169.1 8.1 multiply_convert_fusion.4
  1191.2 7.1 multiply_reduce_fusion.8
  1198.4 8.1 multiply_convert_fusion.4
  1220.5 4.8 multiply_add_fusion.3
  1228.9 14.0 copy.89
  1257.7 5.0 reshape.332
  1262.7 9.4 fusion.103
  1272.1 6.0 reshape.333
  1280.8 10.1 add_convert_fusion.3
  1293.8 5.8 fusion.86
  1306.7 41.0 %all-reduce.11 = (f32[960]{0:T(1024)S(1)}, f32[5280]{0:T(1024)S(1)}) all-reduce(f32[960]{0:T(1024)S(1)} %pad_maximum_fusion.1, f32[5280]{0:T(1024)S(1)} %concatenate.20), channel_id=1, replica_groups=mesh['wide'=8,'narrow'=4] {'wide','narrow'}, use_global_device_ids=true, to_apply=%region_23.24 | all-reduce | flops 6240 | bytes 49920 | tf_op jit(solution)/shard_map/psum | solution.py:245
  1349.7 148.9 %all-reduce.17.cloned.1.call-done = (f32[691200]{0:T(1024)}, f32[230400]{0:T(1024)}, f32[921600]{0:T(1024)}, f32[921600]{0:T(1024)}) async-done(((f32[691200]{0:T(1024)}, f32[230400]{0:T(1024)}, f32[921600]{0:T(1024)}, f32[921600]{0:T(1024)}), (f32[691200]{0:T(1024)}, f32[230400]{0:T(1024)}, f32[921600]{0:T(1024)}, f32[921600]{0:T(1024)})) %all-reduce.17.cloned.1.call-update) | async-done | bytes 11059216
  (543 shorter events, 623.9 us)
Async XLA Ops:
  7.2 6.0 copy-start.31
  7.2 6.8 copy-start.33
  7.2 9.1 copy-start.8
  7.2 141.7 %all-reduce.19.cloned.1.call-start = ((), (), s32[]{:S(2)}) async-start(), calls=%async_computation.3 | async-start | bytes 3686400
  13.1 436.1 %all-gather.5.cloned.1.call-start = ((), (), s32[]{:S(2)}) async-start(), calls=%async_computation | async-start | bytes 3801600 | tf_op jit(solution)/shard_map/all_gather | solution.py:138
  13.9 478.5 %all-gather.7.cloned.1.call-start = ((), (), s32[]{:S(2)}) async-start(), calls=%async_computation.1 | async-start | bytes 3801600 | tf_op jit(solution)/shard_map/all_gather | solution.py:139
  14.7 1483.9 %all-reduce.17.cloned.1.call-start = ((), (), s32[]{:S(2)}) async-start(), calls=%async_computation.2 | async-start | bytes 22118400
  33.6 161.1 %copy-start.28 = (f32[2,1024,12]{1,2,0:T(8,128)}, f32[2,1024,12]{1,2,0:T(8,128)S(1)}, u32[]{:S(2)}) copy-start(f32[2,1024,12]{1,2,0:T(8,128)S(1)} %get-tuple-element.368) | copy-start | bytes 294916
  33.6 161.1 %copy-start.30 = (f32[2,1024,12]{1,2,0:T(8,128)}, f32[2,1024,12]{1,2,0:T(8,128)S(1)}, u32[]{:S(2)}) copy-start(f32[2,1024,12]{1,2,0:T(8,128)S(1)} %get-tuple-element.369) | copy-start | bytes 294916
  152.3 8.4 copy-start.24
  185.4 5.9 copy-start.15
  492.4 43.8 %copy-start.65 = (f32[1920]{0:T(1024)S(1)}, f32[1920]{0:T(1024)}, u32[]{:S(2)}) copy-start(f32[1920]{0:T(1024)} %slice.80) | copy-start | bytes 23044
  492.4 43.8 %copy-start.73 = (f32[480]{0:T(512)S(1)}, f32[480]{0:T(512)}, u32[]{:S(2)}) copy-start(f32[480]{0:T(512)} %get-tuple-element.365) | copy-start | bytes 5764
  536.2 44.0 %copy-start.9 = (bf16[2,60,8,1024]{3,2,0,1:T(8,128)(2,1)S(1)}, bf16[2,60,8,1024]{3,2,0,1:T(8,128)(2,1)}, u32[]{:S(2)}) copy-start(bf16[2,60,8,1024]{3,2,0,1:T(8,128)(2,1)} %copy.105) | copy-start | bytes 5898244
  598.0 10.4 copy-start.51
  598.0 10.5 copy-start.3
  609.9 6.7 slice-start
  622.8 9.5 copy-start.5
  622.8 9.5 copy-start.27
  622.8 9.5 copy-start.38
  634.5 7.9 copy-start
  663.8 7.9 copy-start
  693.0 7.9 copy-start
  722.3 7.9 copy-start
  751.5 7.9 copy-start
  780.8 7.9 copy-start
  810.1 7.9 copy-start
  826.0 5.2 copy-start.11
  839.3 7.9 copy-start
  868.6 7.9 copy-start
  897.8 7.9 copy-start
  913.8 5.2 copy-start.11
  927.1 7.9 copy-start
  956.4 7.9 copy-start
  985.6 7.9 copy-start
  1014.9 7.9 copy-start
  1044.2 7.9 copy-start
  1073.4 7.9 copy-start
  1102.7 7.9 copy-start
  1131.9 7.9 copy-start
  1161.2 7.9 copy-start
  1190.5 7.9 copy-start
  1280.8 11.6 copy-start.25
  1293.8 5.9 copy-start.55
  1304.0 44.5 %copy-start.62 = (f32[960]{0:T(1024)S(1)}, f32[960]{0:T(1024)}, u32[]{:S(2)}) copy-start(f32[960]{0:T(1024)} %param.42) | copy-start | bytes 11524
  1304.0 44.4 %copy-start.67 = (f32[960]{0:T(1024)S(1)}, f32[960]{0:T(1024)}, u32[]{:S(2)}) copy-start(f32[960]{0:T(1024)} %param.43) | copy-start | bytes 11524
  1304.0 44.4 %copy-start.68 = (f32[960]{0:T(1024)S(1)}, f32[960]{0:T(1024)}, u32[]{:S(2)}) copy-start(f32[960]{0:T(1024)} %param.44) | copy-start | bytes 11524
  1304.0 45.0 %copy-start.45 = (f32[5280]{0:T(1024)S(1)}, f32[5280]{0:T(1024)}, u32[]{:S(2)}) copy-start(f32[5280]{0:T(1024)} %param.45) | copy-start | bytes 63364
  1304.0 45.0 %copy-start.59 = (f32[5280]{0:T(1024)S(1)}, f32[5280]{0:T(1024)}, u32[]{:S(2)}) copy-start(f32[5280]{0:T(1024)} %param.46) | copy-start | bytes 63364
  1304.0 45.0 %copy-start.60 = (f32[5280]{0:T(1024)S(1)}, f32[5280]{0:T(1024)}, u32[]{:S(2)}) copy-start(f32[5280]{0:T(1024)} %param.47) | copy-start | bytes 63364
  1304.0 194.6 %copy-start.32 = (f32[28800]{0:T(1024)S(1)}, f32[28800]{0:T(1024)}, u32[]{:S(2)}) copy-start(f32[28800]{0:T(1024)} %param.36) | copy-start | bytes 345604
  1304.0 194.6 %copy-start.40 = (f32[28800]{0:T(1024)S(1)}, f32[28800]{0:T(1024)}, u32[]{:S(2)}) copy-start(f32[28800]{0:T(1024)} %param.37) | copy-start | bytes 345604
  1304.0 194.6 %copy-start.41 = (f32[28800]{0:T(1024)S(1)}, f32[28800]{0:T(1024)}, u32[]{:S(2)}) copy-start(f32[28800]{0:T(1024)} %param.38) | copy-start | bytes 345604
  1304.1 196.3 %copy-start.34 = (f32[28800]{0:T(1024)S(1)}, f32[28800]{0:T(1024)}, u32[]{:S(2)}) copy-start(f32[28800]{0:T(1024)} %param.39) | copy-start | bytes 345604
  1304.1 196.3 %copy-start.42 = (f32[28800]{0:T(1024)S(1)}, f32[28800]{0:T(1024)}, u32[]{:S(2)}) copy-start(f32[28800]{0:T(1024)} %param.40) | copy-start | bytes 345604
  1304.1 196.3 %copy-start.43 = (f32[28800]{0:T(1024)S(1)}, f32[28800]{0:T(1024)}, u32[]{:S(2)}) copy-start(f32[28800]{0:T(1024)} %param.41) | copy-start | bytes 345604
  1304.1 198.1 %copy-start.36 = (f32[21600]{0:T(1024)S(1)}, f32[21600]{0:T(1024)}, u32[]{:S(2)}) copy-start(f32[21600]{0:T(1024)} %param.30) | copy-start | bytes 259204
  1304.1 198.1 %copy-start.46 = (f32[21600]{0:T(1024)S(1)}, f32[21600]{0:T(1024)}, u32[]{:S(2)}) copy-start(f32[21600]{0:T(1024)} %param.31) | copy-start | bytes 259204
  1304.1 198.1 %copy-start.47 = (f32[21600]{0:T(1024)S(1)}, f32[21600]{0:T(1024)}, u32[]{:S(2)}) copy-start(f32[21600]{0:T(1024)} %param.32) | copy-start | bytes 259204
  1304.1 199.8 %copy-start.39 = (f32[7200]{0:T(1024)S(1)}, f32[7200]{0:T(1024)}, u32[]{:S(2)}) copy-start(f32[7200]{0:T(1024)} %param.33) | copy-start | bytes 86404
  1304.1 199.8 %copy-start.56 = (f32[7200]{0:T(1024)S(1)}, f32[7200]{0:T(1024)}, u32[]{:S(2)}) copy-start(f32[7200]{0:T(1024)} %param.34) | copy-start | bytes 86404
  1304.2 199.8 %copy-start.57 = (f32[7200]{0:T(1024)S(1)}, f32[7200]{0:T(1024)}, u32[]{:S(2)}) copy-start(f32[7200]{0:T(1024)} %param.35) | copy-start | bytes 86404
  1347.7 157.7 %copy-start.58 = (f32[5280]{0:T(1024)}, f32[5280]{0:T(1024)S(1)}, u32[]{:S(2)}) copy-start(f32[5280]{0:T(1024)S(1)} %get-tuple-element.307) | copy-start | bytes 63364
  1347.7 157.7 %copy-start.69 = (f32[960]{0:T(1024)}, f32[960]{0:T(1024)S(1)}, u32[]{:S(2)}) copy-start(f32[960]{0:T(1024)S(1)} %get-tuple-element.306) | copy-start | bytes 11524
  (73 other events, 207.9 us)
Sparse Core Ops, SparseCore 0:
  13.5 135.3 all-reduce.18
  152.4 60.3 all-gather.4
  216.2 59.3 all-gather.6
  1278.3 220.2 all-reduce.16
where the time goes:
time: 1530 us; the launch traced here: 1510 us
  matrix products  663 us (43%)
  other arithmetic  364 us (24%)
  waiting for transfers between devices  264 us (17%)
  local copies, waits for them, and re-layouts  162 us (11%)
  blocking collectives  41 us (3%)
    unnamed x6, waiting for transfers between devices  264 us
    dot_general x40, matrix products, masked_scores(): jnp.einsum('rie,rje->rij', queries, keys_low, preferred_element_type=jnp....  215 us
    convert_element_type x20, other arithmetic, head_backward(): grad_scores = (attn_probs * (grad_probs - delta_rows)).astype(jnp.bfloat16)  162 us
    dot_general x20, matrix products, head_backward(): jnp.einsum('rij,rie->rje', attn_probs.astype(jnp.bfloat16), grad_heads, p...  91.6 us
    dot_general x20, matrix products, head_forward(): jnp.einsum('rij,rje->rie', attn_probs.astype(jnp.bfloat16), triple[2], pr...  85 us
    reduce_sum x20, other arithmetic, head_forward(): totals = jnp.sum(weighted, axis=-1, keepdims=True)  67.6 us
    dot_general x20, matrix products, head_backward(): jnp.einsum('rij,rie->rje', grad_scores, queries, preferred_element_type=j...  55.6 us
    dot_general x20, matrix products, head_backward(): jnp.einsum('rij,rje->rie', grad_scores, keys_low, preferred_element_type=...  47.5 us
  transfers between devices with their start and end apart: 4, of which 2 were waited for; matrix products, arithmetic and copies ran while one was open for 26% of the time, Pallas kernels for 0%

commit v1 on v0

v1 whole, which is shorter than its diff:
```python
import functools
import math

import jax
import jax.numpy as jnp
import numpy as np
from jax import lax
from jax.experimental import pallas as pl
from jax.experimental.pallas import tpu as pltpu
from jax.sharding import PartitionSpec as P

D = 480
HEAD_DIM = 24
FF = 1920
STEP = 3
AXES = ("wide", "narrow")

GROUP = 128
PER_GROUP = 5
GROUPS = 4
USED = PER_GROUP * HEAD_DIM
WIDTH = GROUPS * GROUP
HALF = HEAD_DIM // 2
BLOCK = 512
FAR = -1e30
LOG2E = math.log2(math.e)
SCALE = HEAD_DIM**-0.5
VMEM_LIMIT = 56 * 2**20
SAFE = 90.0

f32 = jnp.float32
bf16 = jnp.bfloat16


def contract(left, right, left_dim, right_dim):
    return lax.dot_general(
        left, right, (((left_dim,), (right_dim,)), ((), ())), preferred_element_type=f32
    )


def lanes():
    return lax.broadcasted_iota(jnp.int32, (1, GROUP), 1)


def head_lanes(m):
    lane = lanes()
    return (lane >= HEAD_DIM * m) & (lane < HEAD_DIM * (m + 1))


def of_head(x, m):
    return jnp.where(head_lanes(m) | (lanes() >= USED), x, jnp.zeros_like(x))


def same_head():
    rows = lax.broadcasted_iota(jnp.int32, (GROUP, GROUP), 0) // HEAD_DIM
    columns = lax.broadcasted_iota(jnp.int32, (GROUP, GROUP), 1) // HEAD_DIM
    return jnp.where((rows == columns) & (rows < PER_GROUP), 1.0, 0.0).astype(bf16)


def head_sums(product, same):
    high = product.astype(bf16)
    low = (product - high.astype(f32)).astype(bf16)
    return contract(high, same, 1, 0) + contract(low, same, 1, 0)


def normalized(field):
    average = jnp.mean(field, axis=-1, keepdims=True)
    centered = field - average
    spread = jnp.mean(centered * centered, axis=-1, keepdims=True)
    root = lax.rsqrt(spread + 1e-05)
    return centered * root, root


def norm_back(grad, unit, root, gain_row):
    scaled = grad * gain_row
    return root * (
        scaled
        - jnp.mean(scaled, axis=-1, keepdims=True)
        - unit * jnp.mean(scaled * unit, axis=-1, keepdims=True)
    )


def params(n_axes=1):
    return pltpu.CompilerParams(
        vmem_limit_bytes=VMEM_LIMIT, dimension_semantics=("arbitrary",) * n_axes
    )


def whole(shape):
    return pl.BlockSpec(shape, lambda *_: (0,) * len(shape))


def turn_kernel(
    start_ref, tokens_ref, cotangent_ref, norms_ref, trig_ref, info_ref, spread_ref,
    tokens_out, cotangent_out, normed_out, cosine_out, sine_out, query_out, key_out, pad_out,
):
    length = tokens_ref.shape[0]
    start = start_ref[pl.program_id(0)]
    gain, offset = norms_ref[0:1, :], norms_ref[1:2, :]
    step = 256
    for first in range(0, length, step):
        here = slice(first, first + step)
        target = lax.broadcasted_iota(jnp.int32, (step, length), 0) + (first + start)
        target = jnp.where(target >= length, target - length, target)
        source = lax.broadcasted_iota(jnp.int32, (step, length), 1)
        pick = jnp.where(target == source, 1.0, 0.0).astype(bf16)
        turned = jnp.dot(pick, tokens_ref[...], preferred_element_type=f32)
        tokens_out[here, :] = turned.astype(bf16)
        unit, _ = normalized(turned)
        normed_out[here, :] = (unit * gain + offset).astype(bf16)
        cotangent_out[here, :] = jnp.dot(
            pick, cotangent_ref[...], preferred_element_type=f32
        ).astype(bf16)
    for k, out in ((0, cosine_out), (1, sine_out)):
        part = trig_ref[0, 16 * k : 16 * k + 16, :]
        high = part.astype(bf16)
        rest = part - high.astype(f32)
        middle = rest.astype(bf16)
        low = (rest - middle.astype(f32)).astype(bf16)
        grid = spread_ref[0]
        out[...] = contract(high, grid, 0, 0) + contract(middle, grid, 0, 0) + contract(low, grid, 0, 0)
    info = info_ref[0]
    for k, out in ((1, query_out), (2, key_out), (3, pad_out)):
        out[...] = contract(info, spread_ref[k], 0, 0).astype(bf16)


def turn_rows(start, tokens, cotangent, norms, trig, info, spread):
    rows, length, width = tokens.shape
    row = pl.BlockSpec((length, width), lambda r: (r, 0))
    lane = pl.BlockSpec((length, GROUP), lambda r: (r, 0))
    small = pl.BlockSpec((1,) + trig.shape[1:], lambda r: (r, 0, 0))
    small_info = pl.BlockSpec((1,) + info.shape[1:], lambda r: (r, 0, 0))
    tall = jax.ShapeDtypeStruct((rows * length, width), bf16)

    def lane_shape(kind):
        return jax.ShapeDtypeStruct((rows * length, GROUP), kind)

    return pl.pallas_call(
        turn_kernel,
        grid=(rows,),
        in_specs=[
            pl.BlockSpec(memory_space=pltpu.SMEM), row, row, whole(norms.shape), small, small_info,
            whole(spread.shape),
        ],
        out_specs=[row, row, row, lane, lane, lane, lane, lane],
        out_shape=[tall, tall, tall, lane_shape(f32), lane_shape(f32)] + [lane_shape(bf16)] * 3,
        compiler_params=params(),
    )(
        start, tokens.reshape(rows * length, width), cotangent.reshape(rows * length, width), norms,
        trig, info, spread,
    )


def unturn_kernel(start_ref, outputs_ref, grad_ref, outputs_out, grad_out):
    length = outputs_ref.shape[0]
    start = start_ref[pl.program_id(0)]
    grad = grad_ref[...]
    high = grad.astype(bf16)
    low = (grad - high.astype(f32)).astype(bf16)
    step = 256
    for first in range(0, length, step):
        here = slice(first, first + step)
        target = lax.broadcasted_iota(jnp.int32, (step, length), 0) + (first - start)
        target = jnp.where(target < 0, target + length, target)
        source = lax.broadcasted_iota(jnp.int32, (step, length), 1)
        pick = jnp.where(target == source, 1.0, 0.0).astype(bf16)
        outputs_out[here, :] = jnp.dot(
            pick, outputs_ref[...], preferred_element_type=f32
        ).astype(bf16)
        grad_out[here, :] = jnp.dot(pick, high, preferred_element_type=f32) + jnp.dot(
            pick, low, preferred_element_type=f32
        )


def unturn_rows(start, outputs, grad, length):
    total, width = outputs.shape
    row = pl.BlockSpec((length, width), lambda r: (r, 0))
    return pl.pallas_call(
        unturn_kernel,
        grid=(total // length,),
        in_specs=[pl.BlockSpec(memory_space=pltpu.SMEM), row, row],
        out_specs=[row, row],
        out_shape=[
            jax.ShapeDtypeStruct((total, width), bf16),
            jax.ShapeDtypeStruct((total, width), f32),
        ],
        compiler_params=params(),
    )(start, outputs, grad)


def swap_halves(field, forward):
    low_half = lanes() % HEAD_DIM < HALF
    up = pltpu.roll(field, GROUP - HALF, 1)
    down = pltpu.roll(field, HALF, 1)
    if forward:
        return jnp.where(low_half, -up, down)
    return jnp.where(low_half, up, -down)


def project_kernel(
    normed_ref, gathered_ref, order_ref, bias_ref, cosine_ref, sine_ref, query_lanes, key_lanes,
    q_out, k_out, v_out, weight_out,
):
    @pl.when(pl.program_id(0) == 0)
    def _():
        weight_out[...] = jnp.dot(
            order_ref[...], gathered_ref[...], preferred_element_type=f32
        ).astype(bf16)

    cosine, sine = cosine_ref[...], sine_ref[...]
    own = lanes() < USED
    for g in range(GROUPS):
        to = slice(GROUP * g, GROUP * (g + 1))
        for part, out, factor, spare in (
            (0, q_out, SCALE * LOG2E, query_lanes),
            (1, k_out, 1.0, key_lanes),
        ):
            at = slice(WIDTH * part + GROUP * g, WIDTH * part + GROUP * (g + 1))
            mixed = jnp.dot(
                normed_ref[...], weight_out[:, at], preferred_element_type=f32
            ) + bias_ref[:, at]
            turned = mixed * cosine + swap_halves(mixed, True) * sine
            out[:, to] = jnp.where(own, (turned * factor).astype(bf16), spare[...])
    values = slice(2 * WIDTH, 3 * WIDTH)
    v_out[...] = (
        jnp.dot(normed_ref[...], weight_out[:, values], preferred_element_type=f32)
        + bias_ref[:, values]
    ).astype(bf16)


def project(normed, gathered, order, bias, cosine, sine, query_lanes, key_lanes):
    total = normed.shape[0]
    tile = 512

    def tiled(width):
        return pl.BlockSpec((tile, width), lambda t: (t, 0))

    return pl.pallas_call(
        project_kernel,
        grid=(total // tile,),
        in_specs=[
            tiled(D), whole(gathered.shape), whole(order.shape), whole(bias.shape),
            tiled(GROUP), tiled(GROUP), tiled(GROUP), tiled(GROUP),
        ],
        out_specs=[tiled(WIDTH)] * 3 + [whole((D, 3 * WIDTH))],
        out_shape=[jax.ShapeDtypeStruct((total, WIDTH), bf16)] * 3
        + [jax.ShapeDtypeStruct((D, 3 * WIDTH), bf16)],
        compiler_params=params(),
    )(normed, gathered, order, bias, cosine, sine, query_lanes, key_lanes)


def attend_kernel(q_ref, k_ref, v_ref, pad_ref, attended_out, log_out):
    length = q_ref.shape[0]
    same = same_head()
    own = lanes() < USED
    squares = []
    for ref in (q_ref, k_ref):
        kept = jnp.where(own, ref[...], jnp.zeros((), bf16)).astype(f32)
        sums = contract((kept * kept).astype(bf16), same, 1, 0)
        squares.append(jnp.max(sums, axis=0, keepdims=True))
    safe = jnp.max(squares[0] * squares[1]) <= SAFE * SAFE

    def finish(here, total, weight, shift):
        q, k, v = q_ref[here, :].astype(f32), k_ref[here, :].astype(f32), v_ref[here, :].astype(f32)
        own_score = head_sums(jnp.where(own, q * k, 0.0), same)
        extra = pad_ref[here, :].astype(f32) * jnp.exp2(own_score - shift)
        weight = jnp.where(own, weight + extra, 1.0)
        attended_out[here, :] = ((total + extra * v) / weight).astype(bf16)
        log_out[here, :] = shift + jnp.log2(weight)

    @pl.when(safe)
    def _():
        for first in range(0, length, BLOCK):
            here = slice(first, first + BLOCK)
            k = k_ref[here, :]
            values = jnp.concatenate([v_ref[here, :], jnp.ones((BLOCK, GROUP), bf16)], axis=1)
            total = jnp.zeros((BLOCK, GROUP), f32)
            weight = jnp.zeros((BLOCK, GROUP), f32)
            for m in range(PER_GROUP):
                scores = contract(of_head(q_ref[here, :], m), k, 1, 1)
                probs = jnp.exp2(scores).astype(bf16)
                got = jnp.dot(probs, values, preferred_element_type=f32)
                total = jnp.where(head_lanes(m), got[:, :GROUP], total)
                weight = jnp.where(head_lanes(m), got[:, GROUP:], weight)
            finish(here, total, weight, jnp.zeros((BLOCK, GROUP), f32))

    @pl.when(jnp.logical_not(safe))
    def _():
        for first in range(0, length, BLOCK):
            here = slice(first, first + BLOCK)
            k = k_ref[here, :]
            values = jnp.concatenate([v_ref[here, :], jnp.ones((BLOCK, GROUP), bf16)], axis=1)
            own_score = head_sums(
                jnp.where(own, q_ref[here, :].astype(f32) * k.astype(f32), 0.0), same
            )
            own_score = jnp.where(pad_ref[here, :].astype(f32) > 0.5, own_score, FAR)

            def one_head(m, carry):
                total, weight, shift = carry
                scores = contract(of_head(q_ref[here, :], m), k, 1, 1)
                diagonal = jnp.where(head_lanes(m), own_score, FAR)
                highest = jnp.maximum(
                    jnp.max(scores, axis=1, keepdims=True),
                    jnp.max(diagonal, axis=1, keepdims=True),
                )
                probs = jnp.exp2(scores - highest).astype(bf16)
                got = jnp.dot(probs, values, preferred_element_type=f32)
                return (
                    jnp.where(head_lanes(m), got[:, :GROUP], total),
                    jnp.where(head_lanes(m), got[:, GROUP:], weight),
                    jnp.where(head_lanes(m), highest, shift),
                )

            zero = jnp.zeros((BLOCK, GROUP), f32)
            total, weight, shift = lax.fori_loop(0, PER_GROUP, one_head, (zero, zero, zero))
            finish(here, total, weight, shift)


def attend(q, k, v, pad, length):
    total = q.shape[0]
    block = pl.BlockSpec((length, GROUP), lambda r, g: (r, g))
    pads = pl.BlockSpec((length, GROUP), lambda r, g: (r, 0))
    return pl.pallas_call(
        attend_kernel,
        grid=(total // length, GROUPS),
        in_specs=[block, block, block, pads],
        out_specs=[block, block],
        out_shape=[
            jax.ShapeDtypeStruct((total, WIDTH), bf16),
            jax.ShapeDtypeStruct((total, WIDTH), f32),
        ],
        compiler_params=params(2),
    )(q, k, v, pad)


def attend_back_kernel(
    q_ref, k_ref, v_ref, grad_ref, attended_ref, log_ref, pad_ref, cosine_ref, sine_ref,
    q_out, k_out, v_out,
):
    length = q_ref.shape[0]
    same = same_head()
    own = lanes() < USED
    for first in range(0, length, BLOCK):
        here = slice(first, first + BLOCK)
        q, k, v, grad = q_ref[here, :], k_ref[here, :], v_ref[here, :], grad_ref[here, :]
        logs = log_ref[here, :]
        qf = jnp.where(own, q.astype(f32), 0.0)
        kf = jnp.where(own, k.astype(f32), 0.0)
        vf, gf = v.astype(f32), grad.astype(f32)
        delta = head_sums(gf * attended_ref[here, :].astype(f32), same)
        q_flat = q.astype(f32).T.astype(bf16)
        grad_flat = gf.T.astype(bf16)
        signals, k_heads, grad_keys, grad_values = [], [], [], []
        for m in range(PER_GROUP):
            at = slice(HEAD_DIM * m, HEAD_DIM * (m + 1))
            column = slice(HEAD_DIM * m, HEAD_DIM * m + 1)
            k_head = of_head(k, m)
            scores = contract(q, k_head, 1, 1)
            probs = jnp.exp2(scores - logs[:, column])
            grad_probs = contract(grad, of_head(v, m), 1, 1)
            signal = (probs * (grad_probs - delta[:, column])).astype(bf16)
            grad_values.append(contract(grad_flat[at, :], probs.astype(bf16), 1, 0))
            grad_keys.append(contract(q_flat[at, :], signal, 1, 0))
            signals.append(signal)
            k_heads.append(k_head)
        grad_q = jnp.dot(
            jnp.concatenate(signals, axis=1), jnp.concatenate(k_heads, axis=0), preferred_element_type=f32
        )
        spare = jnp.zeros((GROUP - USED, BLOCK), f32)
        grad_k = jnp.concatenate(grad_keys + [spare], axis=0).T
        grad_v = jnp.concatenate(grad_values + [spare], axis=0).T
        own_score = head_sums(qf * kf, same)
        own_prob = pad_ref[here, :].astype(f32) * jnp.exp2(own_score - logs)
        own_signal = own_prob * (head_sums(gf * vf, same) - delta)
        grad_q = grad_q + own_signal * kf
        grad_k = grad_k + own_signal * qf
        grad_v = grad_v + own_prob * gf
        cosine, sine = cosine_ref[here, :], sine_ref[here, :]
        grad_q = jnp.where(own, grad_q, 0.0)
        q_out[here, :] = (
            SCALE * (grad_q * cosine + swap_halves(grad_q, False) * sine)
        ).astype(bf16)
        k_out[here, :] = (
            (1.0 / LOG2E) * (grad_k * cosine + swap_halves(grad_k, False) * sine)
        ).astype(bf16)
        v_out[here, :] = jnp.where(own, grad_v, 0.0).astype(bf16)


def attend_back(q, k, v, grad, attended, logs, pad, cosine, sine, length):
    total = q.shape[0]
    block = pl.BlockSpec((length, GROUP), lambda r, g: (r, g))
    row = pl.BlockSpec((length, GROUP), lambda r, g: (r, 0))
    return pl.pallas_call(
        attend_back_kernel,
        grid=(total // length, GROUPS),
        in_specs=[block] * 6 + [row] * 3,
        out_specs=[block] * 3,
        out_shape=[jax.ShapeDtypeStruct((total, WIDTH), bf16)] * 3,
        compiler_params=params(2),
    )(q, k, v, grad, attended, logs, pad, cosine, sine)


def gelu_both(v):
    e = jnp.exp2(v * v * (-0.5 * LOG2E))
    t = 1.0 / (1.0 + (0.3275911 / math.sqrt(2.0)) * jnp.abs(v))
    poly = t * (0.5 * 1.061405429) + (0.5 * -1.453152027)
    poly = poly * t + (0.5 * 1.421413741)
    poly = poly * t + (0.5 * -0.284496736)
    poly = poly * t + (0.5 * 0.254829592)
    tail = poly * t * e
    phi = jnp.where(v >= 0.0, 1.0 - tail, tail)
    return v * phi, phi + v * e * (1.0 / math.sqrt(2.0 * math.pi))


UP_AT, DOWN_AT, OUT_AT = 0, FF, FF + 4 * 512
PACK = FF + 4 * 512 + 512
CHUNK = 640


def feed_kernel(
    attended_ref, tokens_ref, cotangent_ref, gathered_ref, order_ref, group_order_ref, rows_ref, up_bias_ref,
    outputs_out, grad_middle_out, grad_attended_out, grads_out, sums_out,
    w_out, w_up, w_down, w_tall, d_out, d_up, d_down,
):
    step = pl.program_id(0)

    @pl.when(step == 0)
    def _():
        order = order_ref[...]
        w_up[...] = jnp.dot(
            order, gathered_ref[:, UP_AT : UP_AT + FF], preferred_element_type=f32
        ).astype(bf16)
        for m in range(4):
            at = DOWN_AT + 512 * m
            part = jnp.dot(order, gathered_ref[:, at : at + 512], preferred_element_type=f32)
            for c in range(0, 512, GROUP):
                w_tall[c // GROUP, pl.ds(m, D, stride=4), :] = part[:, c : c + GROUP]
        for c in range(4):
            n = min(GROUP, D - GROUP * c)
            w_down[:, GROUP * c : GROUP * c + n] = w_tall[c, :, :n].astype(bf16)
        w_out[...] = jnp.dot(
            group_order_ref[...], gathered_ref[:, OUT_AT : OUT_AT + 512], preferred_element_type=f32
        )[:, :D].astype(bf16)
        d_out[...] = jnp.zeros_like(d_out)
        d_up[...] = jnp.zeros_like(d_up)
        d_down[...] = jnp.zeros_like(d_down)
        sums_out[...] = jnp.zeros_like(sums_out)

    attended = attended_ref[...]
    cotangent = cotangent_ref[...]
    out_bias, gain, offset, down_bias = (rows_ref[i : i + 1, :] for i in range(4))
    middle = (
        tokens_ref[...].astype(f32)
        + jnp.dot(attended, w_out[...], preferred_element_type=f32)
        + out_bias
    )
    unit, root = normalized(middle)
    normed = (unit * gain + offset).astype(bf16)
    result = middle + down_bias
    grad_normed = jnp.zeros_like(middle)
    for first in range(0, FF, CHUNK):
        at = slice(first, first + CHUNK)
        hidden = (
            jnp.dot(normed, w_up[:, at], preferred_element_type=f32) + up_bias_ref[:, at]
        )
        active, slope = gelu_both(hidden)
        active = active.astype(bf16)
        result = result + jnp.dot(active, w_down[at, :], preferred_element_type=f32)
        grad_hidden = (contract(cotangent, w_down[at, :], 1, 1) * slope).astype(bf16)
        d_down[at, :] += contract(active, cotangent, 0, 0)
        d_up[:, at] += contract(normed, grad_hidden, 0, 0)
        grad_normed = grad_normed + contract(grad_hidden, w_up[:, at], 1, 1)
        sums_out[0:1, at] += jnp.sum(grad_hidden.astype(f32), axis=0, keepdims=True)
    outputs_out[...] = result.astype(bf16)
    grad_middle = cotangent.astype(f32) + norm_back(grad_normed, unit, root, gain)
    grad_middle_out[...] = grad_middle
    grad_branch = grad_middle.astype(bf16)
    d_out[...] += contract(attended, grad_branch, 0, 0)
    grad_attended_out[...] = contract(grad_branch, w_out[...], 1, 1).astype(bf16)
    for i, terms in enumerate(
        (cotangent.astype(f32), grad_branch.astype(f32), grad_normed * unit, grad_normed)
    ):
        sums_out[i + 1 : i + 2, :D] += jnp.sum(terms, axis=0, keepdims=True)

    @pl.when(step == pl.num_programs(0) - 1)
    def _():
        order = order_ref[...]
        grads_out[:, UP_AT : UP_AT + FF] = contract(order, d_up[...].astype(bf16), 0, 0).astype(bf16)
        for c in range(4):
            n = min(GROUP, D - GROUP * c)
            w_tall[c, :, :n] = d_down[:, GROUP * c : GROUP * c + n]
        for m in range(4):
            for c in range(4):
                at = DOWN_AT + 512 * m + GROUP * c
                part = w_tall[c, pl.ds(m, D, stride=4), :].astype(bf16)
                grads_out[:, at : at + GROUP] = contract(order, part, 0, 0).astype(bf16)
        grads_out[:, OUT_AT : OUT_AT + D] = contract(
            group_order_ref[...], d_out[...].astype(bf16), 0, 0
        ).astype(bf16)
        grads_out[:, OUT_AT + D :] = jnp.zeros_like(grads_out[:, OUT_AT + D :])


def feed(attended, tokens, cotangent, gathered, order, group_order, rows, up_bias):
    total = tokens.shape[0]
    tile = 512

    def tiled(width):
        return pl.BlockSpec((tile, width), lambda t: (t, 0))

    slots = order.shape[1]
    return pl.pallas_call(
        feed_kernel,
        grid=(total // tile,),
        in_specs=[
            tiled(WIDTH), tiled(D), tiled(D), whole(gathered.shape), whole(order.shape),
            whole(group_order.shape), whole(rows.shape), whole(up_bias.shape),
        ],
        out_specs=[tiled(D), tiled(D), tiled(WIDTH), whole((slots, PACK)), whole((8, FF))],
        out_shape=[
            jax.ShapeDtypeStruct((total, D), bf16),
            jax.ShapeDtypeStruct((total, D), f32),
            jax.ShapeDtypeStruct((total, WIDTH), bf16),
            jax.ShapeDtypeStruct((slots, PACK), bf16),
            jax.ShapeDtypeStruct((8, FF), f32),
        ],
        scratch_shapes=[
            pltpu.VMEM((WIDTH, D), bf16),
            pltpu.VMEM((D, FF), bf16),
            pltpu.VMEM((FF, D), bf16),
            pltpu.VMEM((4, FF, GROUP), f32),
            pltpu.VMEM((WIDTH, D), f32),
            pltpu.VMEM((D, FF), f32),
            pltpu.VMEM((FF, D), f32),
        ],
        compiler_params=params(),
    )(attended, tokens, cotangent, gathered, order, group_order, rows, up_bias)


def project_back_kernel(
    dq_ref, dk_ref, dv_ref, normed_ref, tokens_ref, grad_middle_ref, weight_ref, order_ref, gain_ref,
    grad_out, grads_out, sums_out, d_weight,
):
    step = pl.program_id(0)

    @pl.when(step == 0)
    def _():
        d_weight[...] = jnp.zeros_like(d_weight)
        sums_out[...] = jnp.zeros_like(sums_out)

    grad_normed = jnp.zeros(tokens_ref.shape, f32)
    for i, ref in enumerate((dq_ref, dk_ref, dv_ref)):
        at = slice(WIDTH * i, WIDTH * (i + 1))
        grad = ref[...]
        d_weight[:, at] += contract(normed_ref[...], grad, 0, 0)
        grad_normed = grad_normed + contract(grad, weight_ref[:, at], 1, 1)
        sums_out[0:1, at] += jnp.sum(grad.astype(f32), axis=0, keepdims=True)
    unit, root = normalized(tokens_ref[...].astype(f32))
    grad_out[...] = grad_middle_ref[...] + norm_back(grad_normed, unit, root, gain_ref[0:1, :])
    sums_out[1:2, :D] += jnp.sum(grad_normed * unit, axis=0, keepdims=True)
    sums_out[2:3, :D] += jnp.sum(grad_normed, axis=0, keepdims=True)

    @pl.when(step == pl.num_programs(0) - 1)
    def _():
        grads_out[...] = contract(order_ref[...], d_weight[...].astype(bf16), 0, 0).astype(bf16)


def project_back(dq, dk, dv, normed, tokens, grad_middle, weight, order, norms):
    total = tokens.shape[0]
    tile = 512

    def tiled(width):
        return pl.BlockSpec((tile, width), lambda t: (t, 0))

    slots = order.shape[1]
    return pl.pallas_call(
        project_back_kernel,
        grid=(total // tile,),
        in_specs=[tiled(WIDTH)] * 3
        + [tiled(D)] * 3
        + [whole(weight.shape), whole(order.shape), whole(norms.shape)],
        out_specs=[tiled(D), whole((slots, 3 * WIDTH)), whole((8, 3 * WIDTH))],
        out_shape=[
            jax.ShapeDtypeStruct((total, D), f32),
            jax.ShapeDtypeStruct((slots, 3 * WIDTH), bf16),
            jax.ShapeDtypeStruct((8, 3 * WIDTH), f32),
        ],
        scratch_shapes=[pltpu.VMEM((D, 3 * WIDTH), f32)],
        compiler_params=params(),
    )(dq, dk, dv, normed, tokens, grad_middle, weight, order, norms)


class Ring:
    def __init__(self, count):
        self.count = count
        self.bits = [1 << b for b in reversed(range(count.bit_length() - 1))]
        self.masks = [0]
        for bit in self.bits:
            self.masks = self.masks + [bit ^ mask for mask in self.masks]

    def swap(self, x, bit):
        return lax.ppermute(x, AXES, [(i, i ^ bit) for i in range(self.count)])

    def gather(self, x):
        for bit in self.bits:
            x = jnp.concatenate([x, self.swap(x, bit)], axis=0)
        return x

    def scatter_sum(self, x):
        for bit in reversed(self.bits):
            half = x.shape[0] // 2
            got = self.swap(x[half:].astype(bf16), bit)
            x = x[:half].astype(f32) + got.astype(f32)
        return x

    def total(self, x):
        for bit in self.bits:
            x = x + self.swap(x, bit)
        return x


def adamw_update(weight, first, second, gradient, learn_rate):
    first_new = 0.5 * first + 0.5 * gradient
    second_new = 0.5 * second + 0.5 * gradient * gradient
    correction = 1.0 - 0.5 ** float(STEP)
    stepped = first_new / correction / (jnp.sqrt(second_new / correction) + 1e-08)
    return (weight - learn_rate * (stepped + 0.01 * weight), first_new, second_new)


def grouped(rows):
    n, width = rows.shape
    split = rows.reshape(n, width // USED, USED)
    return jnp.pad(split, ((0, 0), (0, 0), (0, GROUP - USED))).reshape(n, width // USED * GROUP)


def ungrouped(rows):
    n, width = rows.shape
    return rows.reshape(n, width // GROUP, GROUP)[:, :, :USED].reshape(n, width // GROUP * USED)


def packed_feed(up, down, out):
    n = up.shape[0]
    down = jnp.pad(down.reshape(n, 4, D), ((0, 0), (0, 0), (0, 512 - D))).reshape(n, 4 * 512)
    return jnp.concatenate([up, down, jnp.pad(out, ((0, 0), (0, 512 - D)))], axis=1)


def unpacked_feed(rows):
    n = rows.shape[0]
    down = rows[:, DOWN_AT : DOWN_AT + 4 * 512].reshape(n, 4, 512)[:, :, :D].reshape(n, FF)
    return rows[:, :FF], down, rows[:, OUT_AT : OUT_AT + D]


def pad_rows(rows, to):
    return jnp.pad(rows, ((0, to - rows.shape[0]), (0, 0)))


def shards(
    devices, tokens, segment_ids, pad_mask, cotangent,
    qkv_weight, qkv_first, qkv_second, out_weight, out_first, out_second,
    up_weight, up_first, up_second, down_weight, down_first, down_second,
    gains, gain_first, gain_second, biases, bias_first, bias_second,
):
    row_count, length, _ = tokens.shape
    ring = Ring(devices)
    own_rows = out_weight.shape[0] // D
    by_rows = out_weight.shape[0] % D == 0
    if by_rows:
        slot = -(-own_rows // 16) * 16
        me = lax.axis_index(AXES)
        qkv_rows = grouped(qkv_weight.astype(bf16).reshape(own_rows, 3 * D))
        qkv_all = ring.gather(pad_rows(qkv_rows, slot))
        feed_rows = packed_feed(
            up_weight.astype(bf16).reshape(own_rows, FF),
            down_weight.astype(bf16).reshape(own_rows, FF),
            out_weight.astype(bf16).reshape(own_rows, D),
        )
        feed_all = ring.gather(pad_rows(feed_rows, slot))
        slots = slot * devices
        place = np.arange(slots)
        masks = jnp.asarray(np.asarray(ring.masks)[place // slot], jnp.int32)
        inner = place % slot
        held = jnp.where(inner < own_rows, (me ^ masks) * own_rows + inner, -1)[None, :]
    else:
        def fetch(weight, width):
            flat = lax.all_gather(weight.astype(bf16), AXES, axis=0, tiled=True)
            return flat.reshape(D, width)

        qkv_all = grouped(fetch(qkv_weight, 3 * D))
        feed_all = packed_feed(fetch(up_weight, FF), fetch(down_weight, FF), fetch(out_weight, D))
        held = jnp.arange(D)[None, :]
    order = (jnp.arange(D)[:, None] == held).astype(bf16)
    wide_row = np.arange(WIDTH)
    wide_row = np.where(wide_row % GROUP < USED, wide_row // GROUP * USED + wide_row % GROUP, -2)
    group_order = (jnp.asarray(wide_row, jnp.int32)[:, None] == held).astype(bf16)

    kinds = jnp.arange(4, dtype=jnp.int32)
    counts = jnp.sum((segment_ids[:, None, :] == kinds[None, :, None]).astype(jnp.int32), axis=2)
    begins = jnp.sum(
        jnp.where(kinds[None, :, None] > kinds[None, None, :], counts[:, None, :], 0), axis=2
    )
    start = jnp.sum(jnp.where(kinds[None, :] == jnp.argmax(counts, axis=1)[:, None], begins, 0), axis=1)
    place = (jnp.arange(length, dtype=jnp.int32)[None, :] + start[:, None]) % length
    among = place[:, None, :] >= begins[:, :, None]
    position = place - jnp.max(jnp.where(among, begins[:, :, None], 0), axis=1)
    segment = jnp.sum(among.astype(jnp.int32), axis=1) - 1
    twice = jnp.concatenate([pad_mask, pad_mask], axis=1)
    present = jnp.stack(
        [lax.dynamic_slice(twice[r], (start[r],), (length,)) for r in range(row_count)]
    ) == 1
    frequency = jnp.exp(jnp.arange(HALF).astype(f32) * (-math.log(10000.0) / HALF))
    phases = position.astype(f32)[:, None, :] * jnp.pad(frequency, (0, 16 - HALF))[None, :, None]
    trig = jnp.concatenate([jnp.cos(phases), jnp.sin(phases)], axis=1)
    is_kind = segment[:, None, :] == kinds[None, :, None]
    info = jnp.concatenate(
        [
            is_kind.astype(f32),
            jnp.where(is_kind & present[:, None, :], 0.0, FAR),
            jnp.where(present, 0.0, 1.0)[:, None, :],
            jnp.zeros((row_count, 7, length), f32),
        ],
        axis=1,
    ).astype(bf16)
    lane = np.arange(GROUP)
    entry = np.arange(16)[:, None]
    spread = np.stack(
        [
            (lane < USED) & (entry == lane % HALF),
            (lane >= USED) & (lane < USED + 4) & (entry == lane - USED),
            (lane >= USED) & (lane < USED + 4) & (entry == lane - USED + 4),
            entry == 8 + 0 * lane,
        ]
    )
    spread = jnp.asarray(spread, bf16)
    norms = jnp.stack([gains[:D], biases[:D]])
    tokens_low, cotangent_low, normed, cosine, sine, query_lanes, key_lanes, pad = turn_rows(
        start, tokens, cotangent, norms, trig, info, spread
    )

    qkv_bias = grouped(biases[D : 4 * D].reshape(1, 3 * D))
    q, k, v, qkv_wide = project(
        normed, qkv_all, order, qkv_bias, cosine, sine, query_lanes, key_lanes
    )
    attended, logs = attend(q, k, v, pad, length)
    rows = jnp.stack(
        [biases[4 * D : 5 * D], gains[D:], biases[5 * D : 6 * D], biases[6 * D + FF :]]
    )
    outputs_low, grad_middle, grad_attended, feed_grads, feed_sums = feed(
        attended, tokens_low, cotangent_low, feed_all, order, group_order, rows,
        biases[6 * D : 6 * D + FF].reshape(1, FF),
    )
    dq, dk, dv = attend_back(
        q, k, v, grad_attended, attended, logs, pad, cosine, sine, length
    )
    grad_tokens, qkv_grads, qkv_sums = project_back(
        dq, dk, dv, normed, tokens_low, grad_middle, qkv_wide, order, norms
    )
    outputs, input_grad = unturn_rows(start, outputs_low, grad_tokens, length)
    outputs = outputs.reshape(tokens.shape)
    input_grad = input_grad.reshape(tokens.shape)

    if by_rows:
        feed_part = ring.scatter_sum(feed_grads)[:own_rows]
        qkv_part = ring.scatter_sum(qkv_grads)[:own_rows]
        up_grad, down_grad, out_grad = (part.reshape(-1) for part in unpacked_feed(feed_part))
        qkv_grad = ungrouped(qkv_part).reshape(-1)
    else:
        def reduce(part):
            return lax.psum_scatter(
                part.astype(f32).reshape(-1), AXES, scatter_dimension=0, tiled=True
            )

        up_grad, down_grad, out_grad = (reduce(part) for part in unpacked_feed(feed_grads))
        qkv_grad = reduce(ungrouped(qkv_grads))
    feed_sums = ring.total(feed_sums)
    qkv_sums = ring.total(qkv_sums)
    gain_grad = jnp.concatenate([qkv_sums[1, :D], feed_sums[3, :D]])
    bias_grad = jnp.concatenate(
        [
            qkv_sums[2, :D], ungrouped(qkv_sums[0:1])[0], feed_sums[2, :D], feed_sums[4, :D],
            feed_sums[0], feed_sums[1, :D],
        ]
    )
    down_bias_grad = bias_grad[6 * D + FF :]
    return (
        outputs,
        input_grad,
        qkv_grad,
        *adamw_update(qkv_weight, qkv_first, qkv_second, qkv_grad, 0.05),
        out_grad,
        *adamw_update(out_weight, out_first, out_second, out_grad, 0.3),
        up_grad,
        *adamw_update(up_weight, up_first, up_second, up_grad, 0.05),
        down_grad,
        *adamw_update(down_weight, down_first, down_second, down_grad, 0.03),
        gain_grad,
        *adamw_update(gains, gain_first, gain_second, gain_grad, 0.2),
        bias_grad,
        *adamw_update(biases, bias_first, bias_second, bias_grad, 0.1),
        down_bias_grad,
    )


def solution(mesh):
    split, copied = P(AXES), P()
    rows, row = P(AXES, None, None), P(AXES, None)
    in_specs = (rows, row, row, rows) + (split,) * 12 + (copied,) * 6
    out_specs = (rows, rows) + (split,) * 16 + (copied,) * 9
    devices = math.prod(mesh.shape[axis] for axis in AXES)
    return jax.shard_map(
        functools.partial(shards, devices),
        mesh=mesh,
        in_specs=in_specs,
        out_specs=out_specs,
        check_vma=False,
    )
```

time: 1530 us -> 423 us (0.28)
  matrix products: 663 us -> 0 us
  other arithmetic: 364 us -> 19.9 us
  Pallas kernels: 0 us -> 211 us
  waiting for transfers between devices: 264 us -> 105 us
  local copies, waits for them, and re-layouts: 162 us -> 36.1 us
  blocking collectives: 41 us -> 0 us
  starting transfers between devices: 0.16 us -> 37.9 us
    dot_general x152 -> x0, matrix products: 663 us -> none  [the longest x40 215 us: masked_scores(): jnp.einsum('rie,rje->rij', queries, keys_low, preferred_element_type=jnp....]
    unnamed x6 -> x0, waiting for transfers between devices: 264 us -> none
    pallas_call x0 -> x7, Pallas kernels: none -> 211 us  [the longest x1 63 us: attend_back(): pl.pallas_call(attend_back_kernel, grid=(total // length, GROUPS), in_spe...]
    convert_element_type x25 -> x7, other arithmetic: 163 us -> 5.59 us  [the longest x1 1.04 us: shards(): qkv_rows = grouped(qkv_weight.astype(bf16).reshape(own_rows, 3 * D))]
    ppermute x0 -> x30, waiting for transfers between devices: none -> 105 us  [swap(): return lax.ppermute(x, AXES, [(i, i ^ bit) for i in range(self.count)])]
    all_gather x2 -> x0, other arithmetic: 79.5 us -> none  [the longest x1 39.9 us: shards(): lax.all_gather(down_weight.astype(jnp.bfloat16), ('wide', 'narrow'), axis...]
    reduce_sum x28 -> x4, other arithmetic: 76.6 us -> 0.6 us  [the longest x1 0.18 us: shards(): jnp.sum(jnp.where(kinds[None, :] == jnp.argmax(counts, axis=1)[:, None],...]
    reshape x14 -> x7, local copies, waits for them, and re-layouts: 60 us -> 1 us  [the longest x1 0.6 us: shards(): biases[6 * D:6 * D + FF].reshape(1, FF)]
  transfers between devices with their start and end apart: 4 -> 30, of which waited for: 2 -> 17; matrix products, arithmetic and copies ran while one was open for 26% -> 11% of each run, Pallas kernels for 0% -> 37%
where the time goes in v1:
time: 423 us; the launch traced here: 415 us
  Pallas kernels  211 us (50%)
  waiting for transfers between devices  105 us (25%)
  starting transfers between devices  37.9 us (9%)
  local copies, waits for them, and re-layouts  36.1 us (9%)
  other arithmetic  19.9 us (5%)
  between operations  5.67 us (1%)
    ppermute x30, waiting for transfers between devices, swap(): return lax.ppermute(x, AXES, [(i, i ^ bit) for i in range(self.count)])  105 us
    pallas_call x1, Pallas kernels, attend_back(): pl.pallas_call(attend_back_kernel, grid=(total // length, GROUPS), in_spe...  63 us
    pallas_call x1, Pallas kernels, feed(): pl.pallas_call(feed_kernel, grid=(total // tile,), in_specs=[tiled(WIDTH)...  55.6 us
    pallas_call x1, Pallas kernels, attend(): pl.pallas_call(attend_kernel, grid=(total // length, GROUPS), in_specs=[b...  45.6 us
    ppermute x30, starting transfers between devices, swap(): return lax.ppermute(x, AXES, [(i, i ^ bit) for i in range(self.count)])  37.9 us
    unnamed x93, local copies, waits for them, and re-layouts  24.9 us
    pallas_call x1, Pallas kernels, project_back(): pl.pallas_call(project_back_kernel, grid=(total // tile,), in_specs=[tile...  14.9 us
    pallas_call x1, Pallas kernels, project(): pl.pallas_call(project_kernel, grid=(total // tile,), in_specs=[tiled(D),...  11.7 us
  transfers between devices with their start and end apart: 30, of which 17 were waited for; matrix products, arithmetic and copies ran while one was open for 11% of the time, Pallas kernels for 37%

profile of v1, /device:TPU:0, one launch (start us, length us, event | category | flops | bytes accessed | tf_op | source)
XLA Modules:
  0.0 415.1 jit_solution(9972906245869413613)
XLA Ops:
  0.7 1.0 convert_element_type.101
  2.6 4.0 collective-permute-start
  6.7 0.8 convert_element_type.105
  7.5 0.9 convert_element_type.103
  8.5 0.9 convert_element_type.104
  9.7 0.7 constant_dynamic-update-slice_fusion.17
  18.8 2.6 copy.62
  21.4 3.9 copy.63
  26.1 2.0 collective-permute-start.6
  29.4 9.8 %shard_map.466 = (bf16[2048,480]{1,0:T(8,128)(2,1)}, bf16[2048,480]{1,0:T(8,128)(2,1)}, bf16[2048,480]{1,0:T(8,128)(2,1)}, f32[2048,128]{1,0:T(8,128)}, f32[2048...) custom-call(s32[2]{0:T(128)} %copy-done.22, ...), custom_call_target="tpu_custom_call" | custom-call | tf_op jit(solution)/shard_map/pallas_call | solution.py:138
  39.2 1.6 collective-permute-start.7
  42.0 11.1 %collective-permute-done.7 = bf16[64,4480]{1,0:T(8,128)(2,1)S(1)} collective-permute-done((bf16[64,4480]{1,0:T(8,128)(2,1)S(1)}, bf16[64,4480]{1,0:T(8,128)(2,1)S(1)}, u32[]{:S(2)}, u32[]{:S(2)}) %collective-permute-start.7) | collective-permute-done | bytes 573472 | tf_op jit(solution)/shard_map/ppermute | solution.py:601
  53.3 1.6 collective-permute-start.8
  54.9 0.9 constant_dynamic-update-slice_fusion.15
  55.8 1.1 constant_dynamic-update-slice_fusion.14
  56.9 21.7 %collective-permute-done.8 = bf16[128,4480]{1,0:T(8,128)(2,1)S(1)} collective-permute-done((bf16[128,4480]{1,0:T(8,128)(2,1)S(1)}, bf16[128,4480]{1,0:T(8,128)(2,1)S(1)}, u32[]{:S(2)}, u32[]{:S(2)}) %collective-permute-start.8) | collective-permute-done | bytes 1146912 | tf_op jit(solution)/shard_map/ppermute | solution.py:601
  78.6 1.5 constant_dynamic-update-slice_fusion.13
  80.3 1.6 collective-permute-start.2
  82.4 5.2 %collective-permute-done.2 = bf16[64,1536]{1,0:T(8,128)(2,1)S(1)} collective-permute-done((bf16[64,1536]{1,0:T(8,128)(2,1)S(1)}, bf16[64,1536]{1,0:T(8,128)(2,1)S(1)}, u32[]{:S(2)}, u32[]{:S(2)}) %collective-permute-start.2) | collective-permute-done | bytes 196640 | tf_op jit(solution)/shard_map/ppermute | solution.py:601
  87.6 1.6 collective-permute-start.3
  90.6 7.8 %collective-permute-done.3 = bf16[128,1536]{1,0:T(8,128)(2,1)S(1)} collective-permute-done((bf16[128,1536]{1,0:T(8,128)(2,1)S(1)}, bf16[128,1536]{1,0:T(8,128)(2,1)S(1)}, u32[]{:S(2)}, u32[]{:S(2)}) %collective-permute-start.3) | collective-permute-done | bytes 393248 | tf_op jit(solution)/shard_map/ppermute | solution.py:601
  98.4 0.8 constant_dynamic-update-slice_fusion.2
  99.9 0.9 fusion.order_ref
  100.8 1.0 compare_convert_fusion.group_order_ref
  101.8 0.9 constant_dynamic-update-slice_fusion.7.gathered_ref
  102.7 11.7 %shard_map.467 = (bf16[2048,512]{1,0:T(8,128)(2,1)}, bf16[2048,512]{1,0:T(8,128)(2,1)}, bf16[2048,512]{1,0:T(8,128)(2,1)}, bf16[480,1536]{1,0:T(8,128)(2,1)}) custom-call(bf16[2048,480]{1,0:T(8,128)(2,1)} %get-tuple-element.56.normed_ref, bf16[512,1536]{1,0:T(8,128)(2,1)} %constant_dynamic-update-slice_fusion.7.gathered_ref, ...), custom_call_target="tpu_custom_call" | custom-call | tf_op jit(solution)/shard_map/pallas_call | solution.py:238
  114.4 45.6 %shard_map.468 = (bf16[2048,512]{1,0:T(8,128)(2,1)}, f32[2048,512]{1,0:T(8,128)}) custom-call(bf16[2048,512]{1,0:T(8,128)(2,1)} %get-tuple-element.61.q_ref, bf16[2048,512]{1,0:T(8,128)(2,1)} %get-tuple-element.62.k_ref, bf16[2048,512]{1,0:T(8,128)(2,1)} %get-tuple-element.63.v_ref, bf16[2048,128]{1,0:T(8,128)(2,1)} %get-tuple-element.64.pad_ref), custom_call_target="tpu_custom_call" | custom-call | tf_op jit(solution)/shard_map/pallas_call | solution.py:323
  160.3 2.2 copy-done
  162.5 55.6 %shard_map.469 = (bf16[2048,480]{1,0:T(8,128)(2,1)}, f32[2048,480]{1,0:T(8,128)}, bf16[2048,512]{1,0:T(8,128)(2,1)}, bf16[512,4480]{1,0:T(8,128)(2,1)}, f32[8,1920]{1,0:T(8,128)}) custom-call(bf16[2048,512]{1,0:T(8,128)(2,1)} %get-tuple-element.65.attended_ref, bf16[2048,480]{1,0:T(8,128)(2,1)} %get-tuple-element.66.tokens_ref, ...), custom_call_target="tpu_custom_call" | custom-call | tf_op jit(solution)/shard_map/pallas_call | solution.py:511
  218.1 3.2 slice.178
  221.9 63.0 %shard_map.470 = (bf16[2048,512]{1,0:T(8,128)(2,1)}, bf16[2048,512]{1,0:T(8,128)(2,1)}, bf16[2048,512]{1,0:T(8,128)(2,1)}) custom-call(bf16[2048,512]{1,0:T(8,128)(2,1)} %get-tuple-element.61.q_ref, bf16[2048,512]{1,0:T(8,128)(2,1)} %get-tuple-element.62.k_ref, bf16[2048,512]{1,0:T(8,128)(2,1)} %get-tuple-element.63.v_ref, ...), custom_call_target="tpu_custom_call" | custom-call | tf_op jit(solution)/shard_map/pallas_call | solution.py:393
  284.8 14.9 %shard_map.471 = (f32[2048,480]{1,0:T(8,128)}, bf16[512,1536]{1,0:T(8,128)(2,1)}, f32[8,1536]{1,0:T(8,128)}) custom-call(bf16[2048,512]{1,0:T(8,128)(2,1)} %get-tuple-element.71.dq_ref, bf16[2048,512]{1,0:T(8,128)(2,1)} %get-tuple-element.72.dk_ref, bf16[2048,512]{1,0:T(8,128)(2,1)} %get-tuple-element.73.dv_ref, ...), custom_call_target="tpu_custom_call" | custom-call | tf_op jit(solution)/shard_map/pallas_call | solution.py:575
  299.8 2.6 collective-permute-start.20
  302.4 3.3 collective-permute-done.20
  305.6 0.8 add.244
  306.5 3.4 collective-permute-start.25
  309.9 1.0 collective-permute-done.21
  310.9 1.4 collective-permute-start.22
  312.3 1.3 collective-permute-start.26
  313.7 1.2 slice.166
  315.1 1.5 collective-permute-start.23
  316.6 1.5 collective-permute-start.27
  318.1 1.1 collective-permute-done.23
  319.3 10.4 %shard_map.472 = (bf16[2048,480]{1,0:T(8,128)(2,1)}, f32[2048,480]{1,0:T(8,128)}) custom-call(s32[2]{0:T(128)} %copy-done.22, bf16[2048,480]{1,0:T(8,128)(2,1)} %get-tuple-element.68.outputs_ref, f32[2048,480]{1,0:T(8,128)} %get-tuple-element.76.grad_ref), custom_call_target="tpu_custom_call" | custom-call | tf_op jit(solution)/shard_map/pallas_call | solution.py:178
  329.7 3.9 copy.64
  333.6 5.3 %copy.65 = f32[2,1024,480]{1,2,0:T(8,128)} copy(f32[2,1024,480]{2,1,0:T(8,128)} %bitcast.39) | data formatting | bytes 7864320
  338.9 1.4 collective-permute-start.28
  340.4 3.0 collective-permute-done.28
  343.6 1.1 collective-permute-done.29
  344.9 1.6 convert_add_fusion.1
  346.5 1.4 collective-permute-start.11
  348.0 2.1 convert_add_fusion
  350.9 7.6 %collective-permute-done.11 = bf16[128,1536]{1,0:T(8,128)(2,1)S(1)} collective-permute-done((bf16[128,1536]{1,0:T(8,128)(2,1)S(1)}, bf16[128,1536]{1,0:T(8,128)(2,1)S(1)}, u32[]{:S(2)}, u32[]{:S(2)}) %collective-permute-start.11) | collective-permute-done | bytes 393248 | tf_op jit(solution)/shard_map/ppermute | solution.py:601
  358.6 1.4 collective-permute-start.12
  360.7 3.7 collective-permute-done.12
  365.2 17.1 %collective-permute-done.16 = bf16[128,4480]{1,0:T(8,128)(2,1)S(1)} collective-permute-done((bf16[128,4480]{1,0:T(8,128)(2,1)S(1)}, bf16[128,4480]{1,0:T(8,128)(2,1)S(1)}, u32[]{:S(2)}, u32[]{:S(2)}) %collective-permute-start.16) | collective-permute-done | bytes 1146912 | tf_op jit(solution)/shard_map/ppermute | solution.py:601
  382.6 1.4 collective-permute-start.17
  384.8 2.1 collective-permute-start.14
  386.9 10.0 %collective-permute-done.17 = bf16[64,4480]{1,0:T(8,128)(2,1)S(1)} collective-permute-done((bf16[64,4480]{1,0:T(8,128)(2,1)S(1)}, bf16[64,4480]{1,0:T(8,128)(2,1)S(1)}, u32[]{:S(2)}, u32[]{:S(2)}) %collective-permute-start.17) | collective-permute-done | bytes 573472 | tf_op jit(solution)/shard_map/ppermute | solution.py:601
  398.1 6.2 %collective-permute-done.18 = bf16[32,4480]{1,0:T(8,128)(2,1)S(1)} collective-permute-done((bf16[32,4480]{1,0:T(8,128)(2,1)S(1)}, bf16[32,4480]{1,0:T(8,128)(2,1)S(1)}, u32[]{:S(2)}, u32[]{:S(2)}) %collective-permute-start.18) | collective-permute-done | bytes 286752 | tf_op jit(solution)/shard_map/ppermute | solution.py:601
  404.5 2.5 collective-permute-start.19
  407.7 4.3 %collective-permute-done.19 = bf16[16,4480]{1,0:T(8,128)(2,1)S(1)} collective-permute-done((bf16[16,4480]{1,0:T(8,128)(2,1)S(1)}, bf16[16,4480]{1,0:T(8,128)(2,1)S(1)}, u32[]{:S(2)}, u32[]{:S(2)}) %collective-permute-start.19) | collective-permute-done | bytes 143392 | tf_op jit(solution)/shard_map/ppermute | solution.py:601
  413.3 0.8 multiply_subtract_fusion
  414.0 0.8 multiply_subtract_fusion.1
  (204 shorter events, 20.0 us)
Async XLA Ops:
  0.7 9.8 %copy-start.26 = (s32[2,1024]{1,0:T(2,128)S(1)}, s32[2,1024]{1,0:T(2,128)}, u32[]{:S(2)}) copy-start(s32[2,1024]{1,0:T(2,128)} %param.28) | copy-start | bytes 24580
  0.7 14.2 %copy-start.15 = (f32[5280]{0:T(1024)S(1)}, f32[5280]{0:T(1024)}, u32[]{:S(2)}) copy-start(f32[5280]{0:T(1024)} %param.46) | copy-start | bytes 63364
  0.7 14.3 %copy-start.25 = (f32[960]{0:T(1024)S(1)}, f32[960]{0:T(1024)}, u32[]{:S(2)}) copy-start(f32[960]{0:T(1024)} %param.43) | copy-start | bytes 11524
  0.7 14.7 %copy-start.21 = (s32[2,1024]{1,0:T(2,128)S(1)}, s32[2,1024]{1,0:T(2,128)}, u32[]{:S(2)}) copy-start(s32[2,1024]{1,0:T(2,128)} %param.29) | copy-start | bytes 24580
  0.7 18.1 %copy-start.1 = (bf16[2,1024,480]{1,2,0:T(8,128)(2,1)S(1)}, bf16[2,1024,480]{1,2,0:T(8,128)(2,1)}, u32[]{:S(2)}) copy-start(bf16[2,1024,480]{1,2,0:T(8,128)(2,1)} %param.27) | copy-start | bytes 5898244
  2.6 38.2 %collective-permute-start = (bf16[16,1536]{1,0:T(8,128)(2,1)S(1)}, bf16[16,1536]{1,0:T(8,128)(2,1)S(1)}, u32[]{:S(2)}, u32[]{:S(2)}) collective-permute-start(bf16[16,1536]{1,0:T(8,128)(2,1)S(1)} %get-tuple-element.212), channel_id=1, source_target_pairs={{0,16},{1,17},{2,18},{3,19},{4,20},{5,21},{6,22},{7,23},{8,24},{9,... | collective-permute-start | bytes 147464 | tf_op jit(solution)/shard_map/ppermute | solution.py:601
  10.4 15.7 %collective-permute-start.5 = (bf16[16,4480]{1,0:T(8,128)(2,1)S(1)}, bf16[16,4480]{1,0:T(8,128)(2,1)S(1)}, u32[]{:S(2)}, u32[]{:S(2)}) collective-permute-start(bf16[16,4480]{1,0:T(8,128)(2,1)S(1)} %get-tuple-element.199), channel_id=1, source_target_pairs={{0,16},{1,17},{2,18},{3,19},{4,20},{5,21},{6,22},{7,23},{8,24},{9,... | collective-permute-start | bytes 430088 | tf_op jit(solution)/shard_map/ppermute | solution.py:601
  11.6 9.8 %copy-start.22 = (s32[2]{0:T(128)}, s32[2]{0:T(128)S(1)}, u32[]{:S(2)}) copy-start(s32[2]{0:T(128)S(1)} %fusion.14.start_ref) | copy-start | bytes 28
  26.1 13.0 %collective-permute-start.6 = (bf16[32,4480]{1,0:T(8,128)(2,1)S(1)}, bf16[32,4480]{1,0:T(8,128)(2,1)S(1)}, u32[]{:S(2)}, u32[]{:S(2)}) collective-permute-start(bf16[32,4480]{1,0:T(8,128)(2,1)S(1)} %pad_maximum_fusion.3), channel_id=1, source_target_pairs={{0,8},{1,9},{2,10},{3,11},{4,12},{5,13},{6,14},{7,15},{8,0},{9,1},... | collective-permute-start | bytes 860168 | tf_op jit(solution)/shard_map/ppermute | solution.py:601
  39.2 13.9 %collective-permute-start.7 = (bf16[64,4480]{1,0:T(8,128)(2,1)S(1)}, bf16[64,4480]{1,0:T(8,128)(2,1)S(1)}, u32[]{:S(2)}, u32[]{:S(2)}) collective-permute-start(bf16[64,4480]{1,0:T(8,128)(2,1)S(1)} %pad_maximum_fusion.1), channel_id=1, source_target_pairs={{0,4},{1,5},{2,6},{3,7},{4,0},{5,1},{6,2},{7,3},{8,12},{9,13},{10,... | collective-permute-start | bytes 1720328 | tf_op jit(solution)/shard_map/ppermute | solution.py:601
  40.8 39.4 %collective-permute-start.1 = (bf16[32,1536]{1,0:T(8,128)(2,1)S(1)}, bf16[32,1536]{1,0:T(8,128)(2,1)S(1)}, u32[]{:S(2)}, u32[]{:S(2)}) collective-permute-start(bf16[32,1536]{1,0:T(8,128)(2,1)S(1)} %pad_maximum_fusion.6), channel_id=1, source_target_pairs={{0,8},{1,9},{2,10},{3,11},{4,12},{5,13},{6,14},{7,15},{8,0},{9,1},... | collective-permute-start | bytes 294920 | tf_op jit(solution)/shard_map/ppermute | solution.py:601
  53.3 25.3 %collective-permute-start.8 = (bf16[128,4480]{1,0:T(8,128)(2,1)S(1)}, bf16[128,4480]{1,0:T(8,128)(2,1)S(1)}, u32[]{:S(2)}, u32[]{:S(2)}) collective-permute-start(bf16[128,4480]{1,0:T(8,128)(2,1)S(1)} %pad_maximum_fusion), channel_id=1, source_target_pairs={{0,2},{1,3},{2,0},{3,1},{4,6},{5,7},{6,4},{7,5},{8,10},{9,11},{10,... | collective-permute-start | bytes 3440648 | tf_op jit(solution)/shard_map/ppermute | solution.py:601
  56.9 24.9 %copy-start.30 = (bf16[256,1536]{1,0:T(8,128)(2,1)S(1)}, bf16[256,1536]{1,0:T(8,128)(2,1)}, u32[]{:S(2)}) copy-start(bf16[256,1536]{1,0:T(8,128)(2,1)} %get-tuple-element.210) | copy-start | bytes 2359300
  80.1 19.7 %copy-start.32 = (s32[512]{0:T(512)S(1)}, s32[512]{0:T(512)}, u32[]{:S(2)}) copy-start(s32[512]{0:T(512)} %constant.115.clone) | copy-start | bytes 6148
  80.1 19.7 %copy-start.33 = (s32[512]{0:T(512)S(1)}, s32[512]{0:T(512)}, u32[]{:S(2)}) copy-start(s32[512]{0:T(512)} %constant.114.clone) | copy-start | bytes 6148
  80.1 19.7 %copy-start.34 = (pred[512]{0:T(512)(128)(4,1)S(1)}, pred[512]{0:T(512)(128)(4,1)}, u32[]{:S(2)}) copy-start(pred[512]{0:T(512)(128)(4,1)} %constant.116.clone) | copy-start | bytes 1540
  80.1 20.7 %copy-start.31 = (s32[512]{0:T(512)S(1)}, s32[512]{0:T(512)}, u32[]{:S(2)}) copy-start(s32[512]{0:T(512)} %constant.117.clone) | copy-start | bytes 6148
  80.1 79.8 %collective-permute-start.9 = (bf16[256,4480]{1,0:T(8,128)(2,1)}, bf16[256,4480]{1,0:T(8,128)(2,1)S(1)}, u32[]{:S(2)}, u32[]{:S(2)}) collective-permute-start(bf16[256,4480]{1,0:T(8,128)(2,1)} %get-tuple-element.185), channel_id=1, source_target_pairs={{0,1},{1,0},{2,3},{3,2},{4,5},{5,4},{6,7},{7,6},{8,9},{9,8},{10,11... | collective-permute-start | bytes 6881288 | tf_op jit(solution)/shard_map/ppermute | solution.py:601
  80.3 7.4 %collective-permute-start.2 = (bf16[64,1536]{1,0:T(8,128)(2,1)S(1)}, bf16[64,1536]{1,0:T(8,128)(2,1)S(1)}, u32[]{:S(2)}, u32[]{:S(2)}) collective-permute-start(bf16[64,1536]{1,0:T(8,128)(2,1)S(1)} %pad_maximum_fusion.5), channel_id=1, source_target_pairs={{0,4},{1,5},{2,6},{3,7},{4,0},{5,1},{6,2},{7,3},{8,12},{9,13},{10,... | collective-permute-start | bytes 589832 | tf_op jit(solution)/shard_map/ppermute | solution.py:601
  87.6 10.8 %collective-permute-start.3 = (bf16[128,1536]{1,0:T(8,128)(2,1)S(1)}, bf16[128,1536]{1,0:T(8,128)(2,1)S(1)}, u32[]{:S(2)}, u32[]{:S(2)}) collective-permute-start(bf16[128,1536]{1,0:T(8,128)(2,1)S(1)} %pad_maximum_fusion.2), channel_id=1, source_target_pairs={{0,2},{1,3},{2,0},{3,1},{4,6},{5,7},{6,4},{7,5},{8,10},{9,11},{10,... | collective-permute-start | bytes 1179656 | tf_op jit(solution)/shard_map/ppermute | solution.py:601
  99.2 2.5 collective-permute-start.4
  101.8 58.2 %slice-start = ((s8[4587520]{0:T(1024)(128)(4,1)}), s8[4194304]{0:T(1024)(128)(4,1)S(1)}, s32[]{:S(2)}) async-start(s8[4587520]{0:T(1024)(128)(4,1)} %bitcast.37), calls=%async_computation | async-start | bytes 8388608
  102.7 57.3 %slice-start.1 = ((s8[4587520]{0:T(1024)(128)(4,1)}), s8[393216]{0:T(1024)(128)(4,1)S(1)}, s32[]{:S(2)}) async-start(s8[4587520]{0:T(1024)(128)(4,1)} %bitcast.37), calls=%async_computation.1 | async-start | bytes 786432
  221.3 126.6 %collective-permute-start.15 = (bf16[256,4480]{1,0:T(8,128)(2,1)}, bf16[256,4480]{1,0:T(8,128)(2,1)S(1)}, u32[]{:S(2)}, u32[]{:S(2)}) collective-permute-start(bf16[256,4480]{1,0:T(8,128)(2,1)} %slice.178), channel_id=1, source_target_pairs={{0,1},{1,0},{2,3},{3,2},{4,5},{5,4},{6,7},{7,6},{8,9},{9,8},{10,11... | collective-permute-start | bytes 6881288 | tf_op jit(solution)/shard_map/ppermute | solution.py:601
  284.8 21.7 %copy-start.18 = (f32[8,1920]{1,0:T(8,128)S(1)}, f32[8,1920]{1,0:T(8,128)}, u32[]{:S(2)}) copy-start(f32[8,1920]{1,0:T(8,128)} %get-tuple-element.82) | copy-start | bytes 184324
  299.8 5.9 %collective-permute-start.20 = (f32[8,1536]{1,0:T(8,128)}, f32[8,1536]{1,0:T(8,128)S(1)}, u32[]{:S(2)}, u32[]{:S(2)}) collective-permute-start(f32[8,1536]{1,0:T(8,128)} %get-tuple-element.81), channel_id=1, source_target_pairs={{0,16},{1,17},{2,18},{3,19},{4,20},{5,21},{6,22},{7,23},{8,24},{9,... | collective-permute-start | bytes 147464 | tf_op jit(solution)/shard_map/ppermute | solution.py:601
  306.4 4.5 %collective-permute-start.21 = (f32[8,1536]{1,0:T(8,128)S(1)}, f32[8,1536]{1,0:T(8,128)S(1)}, u32[]{:S(2)}, u32[]{:S(2)}) collective-permute-start(f32[8,1536]{1,0:T(8,128)S(1)} %add.244), channel_id=1, source_target_pairs={{0,8},{1,9},{2,10},{3,11},{4,12},{5,13},{6,14},{7,15},{8,0},{9,1},... | collective-permute-start | bytes 147464 | tf_op jit(solution)/shard_map/ppermute | solution.py:601
  306.5 5.8 %collective-permute-start.25 = (f32[8,1920]{1,0:T(8,128)S(1)}, f32[8,1920]{1,0:T(8,128)S(1)}, u32[]{:S(2)}, u32[]{:S(2)}) collective-permute-start(f32[8,1920]{1,0:T(8,128)S(1)} %copy-done.18), channel_id=1, source_target_pairs={{0,16},{1,17},{2,18},{3,19},{4,20},{5,21},{6,22},{7,23},{8,24},{9,... | collective-permute-start | bytes 184328 | tf_op jit(solution)/shard_map/ppermute | solution.py:601
  310.9 4.1 collective-permute-start.22
  312.3 4.3 %collective-permute-start.26 = (f32[8,1920]{1,0:T(8,128)S(1)}, f32[8,1920]{1,0:T(8,128)S(1)}, u32[]{:S(2)}, u32[]{:S(2)}) collective-permute-start(f32[8,1920]{1,0:T(8,128)S(1)} %add.249), channel_id=1, source_target_pairs={{0,8},{1,9},{2,10},{3,11},{4,12},{5,13},{6,14},{7,15},{8,0},{9,1},... | collective-permute-start | bytes 184328 | tf_op jit(solution)/shard_map/ppermute | solution.py:601
  314.9 30.0 %collective-permute-start.10 = (bf16[256,1536]{1,0:T(8,128)(2,1)S(1)}, bf16[256,1536]{1,0:T(8,128)(2,1)}, u32[]{:S(2)}, u32[]{:S(2)}) collective-permute-start(bf16[256,1536]{1,0:T(8,128)(2,1)S(1)} %slice.166), channel_id=1, source_target_pairs={{0,1},{1,0},{2,3},{3,2},{4,5},{5,4},{6,7},{7,6},{8,9},{9,8},{10,11... | collective-permute-start | bytes 2359304 | tf_op jit(solution)/shard_map/ppermute | solution.py:601
  315.1 4.2 %collective-permute-start.23 = (f32[8,1536]{1,0:T(8,128)S(1)}, f32[8,1536]{1,0:T(8,128)S(1)}, u32[]{:S(2)}, u32[]{:S(2)}) collective-permute-start(f32[8,1536]{1,0:T(8,128)S(1)} %add.246), channel_id=1, source_target_pairs={{0,2},{1,3},{2,0},{3,1},{4,6},{5,7},{6,4},{7,5},{8,10},{9,11},{10,... | collective-permute-start | bytes 147464 | tf_op jit(solution)/shard_map/ppermute | solution.py:601
  316.6 22.3 %collective-permute-start.27 = (f32[8,1920]{1,0:T(8,128)S(1)}, f32[8,1920]{1,0:T(8,128)S(1)}, u32[]{:S(2)}, u32[]{:S(2)}) collective-permute-start(f32[8,1920]{1,0:T(8,128)S(1)} %add.250), channel_id=1, source_target_pairs={{0,4},{1,5},{2,6},{3,7},{4,0},{5,1},{6,2},{7,3},{8,12},{9,13},{10,... | collective-permute-start | bytes 184328 | tf_op jit(solution)/shard_map/ppermute | solution.py:601
  319.3 21.1 %collective-permute-start.24 = (f32[8,1536]{1,0:T(8,128)S(1)}, f32[8,1536]{1,0:T(8,128)S(1)}, u32[]{:S(2)}, u32[]{:S(2)}) collective-permute-start(f32[8,1536]{1,0:T(8,128)S(1)} %add.247), channel_id=1, source_target_pairs={{0,1},{1,0},{2,3},{3,2},{4,5},{5,4},{6,7},{7,6},{8,9},{9,8},{10,11... | collective-permute-start | bytes 147464 | tf_op jit(solution)/shard_map/ppermute | solution.py:601
  338.9 4.4 %collective-permute-start.28 = (f32[8,1920]{1,0:T(8,128)S(1)}, f32[8,1920]{1,0:T(8,128)S(1)}, u32[]{:S(2)}, u32[]{:S(2)}) collective-permute-start(f32[8,1920]{1,0:T(8,128)S(1)} %add.251), channel_id=1, source_target_pairs={{0,2},{1,3},{2,0},{3,1},{4,6},{5,7},{6,4},{7,5},{8,10},{9,11},{10,... | collective-permute-start | bytes 184328 | tf_op jit(solution)/shard_map/ppermute | solution.py:601
  343.4 1.3 collective-permute-start.29
  344.7 5.3 %copy-start.27 = (f32[1,480]{1,0:T(1,128)}, f32[1,480]{1,0:T(1,128)S(1)}, u32[]{:S(2)}) copy-start(f32[1,480]{1,0:T(1,128)S(1)} %get-tuple-element.202) | copy-start | bytes 5764
  344.8 15.2 %copy-start.14 = (f32[5280]{0:T(1024)}, f32[5280]{0:T(1024)S(1)}, u32[]{:S(2)}) copy-start(f32[5280]{0:T(1024)S(1)} %concatenate.82) | copy-start | bytes 63364
  346.5 12.0 %collective-permute-start.11 = (bf16[128,1536]{1,0:T(8,128)(2,1)S(1)}, bf16[128,1536]{1,0:T(8,128)(2,1)S(1)}, u32[]{:S(2)}, u32[]{:S(2)}) collective-permute-start(bf16[128,1536]{1,0:T(8,128)(2,1)S(1)} %slice.257), channel_id=1, source_target_pairs={{0,2},{1,3},{2,0},{3,1},{4,6},{5,7},{6,4},{7,5},{8,10},{9,11},{10,... | collective-permute-start | bytes 1179656 | tf_op jit(solution)/shard_map/ppermute | solution.py:601
  350.1 10.0 %copy-start.23 = (f32[5280]{0:T(1024)S(1)}, f32[5280]{0:T(1024)}, u32[]{:S(2)}) copy-start(f32[5280]{0:T(1024)} %param.47) | copy-start | bytes 63364
  350.1 10.0 %copy-start.24 = (f32[5280]{0:T(1024)S(1)}, f32[5280]{0:T(1024)}, u32[]{:S(2)}) copy-start(f32[5280]{0:T(1024)} %param.48) | copy-start | bytes 63364
  350.2 32.1 %collective-permute-start.16 = (bf16[128,4480]{1,0:T(8,128)(2,1)S(1)}, bf16[128,4480]{1,0:T(8,128)(2,1)S(1)}, u32[]{:S(2)}, u32[]{:S(2)}) collective-permute-start(bf16[128,4480]{1,0:T(8,128)(2,1)S(1)} %slice.255), channel_id=1, source_target_pairs={{0,2},{1,3},{2,0},{3,1},{4,6},{5,7},{6,4},{7,5},{8,10},{9,11},{10,... | collective-permute-start | bytes 3440648 | tf_op jit(solution)/shard_map/ppermute | solution.py:601
  358.6 5.7 %collective-permute-start.12 = (bf16[64,1536]{1,0:T(8,128)(2,1)S(1)}, bf16[64,1536]{1,0:T(8,128)(2,1)S(1)}, u32[]{:S(2)}, u32[]{:S(2)}) collective-permute-start(bf16[64,1536]{1,0:T(8,128)(2,1)S(1)} %slice.259), channel_id=1, source_target_pairs={{0,4},{1,5},{2,6},{3,7},{4,0},{5,1},{6,2},{7,3},{8,12},{9,13},{10,... | collective-permute-start | bytes 589832 | tf_op jit(solution)/shard_map/ppermute | solution.py:601
  364.4 19.6 %copy-start.28 = (f32[960]{0:T(1024)S(1)}, f32[960]{0:T(1024)}, u32[]{:S(2)}) copy-start(f32[960]{0:T(1024)} %param.44) | copy-start | bytes 11524
  364.5 19.6 %copy-start.29 = (f32[960]{0:T(1024)S(1)}, f32[960]{0:T(1024)}, u32[]{:S(2)}) copy-start(f32[960]{0:T(1024)} %param.45) | copy-start | bytes 11524
  364.5 20.3 %collective-permute-start.13 = (bf16[32,1536]{1,0:T(8,128)(2,1)S(1)}, bf16[32,1536]{1,0:T(8,128)(2,1)S(1)}, u32[]{:S(2)}, u32[]{:S(2)}) collective-permute-start(bf16[32,1536]{1,0:T(8,128)(2,1)S(1)} %slice.261), channel_id=1, source_target_pairs={{0,8},{1,9},{2,10},{3,11},{4,12},{5,13},{6,14},{7,15},{8,0},{9,1},... | collective-permute-start | bytes 294920 | tf_op jit(solution)/shard_map/ppermute | solution.py:601
  382.6 14.3 %collective-permute-start.17 = (bf16[64,4480]{1,0:T(8,128)(2,1)S(1)}, bf16[64,4480]{1,0:T(8,128)(2,1)S(1)}, u32[]{:S(2)}, u32[]{:S(2)}) collective-permute-start(bf16[64,4480]{1,0:T(8,128)(2,1)S(1)} %slice.256), channel_id=1, source_target_pairs={{0,4},{1,5},{2,6},{3,7},{4,0},{5,1},{6,2},{7,3},{8,12},{9,13},{10,... | collective-permute-start | bytes 1720328 | tf_op jit(solution)/shard_map/ppermute | solution.py:601
  384.8 13.0 %collective-permute-start.14 = (bf16[16,1536]{1,0:T(8,128)(2,1)S(1)}, bf16[16,1536]{1,0:T(8,128)(2,1)S(1)}, u32[]{:S(2)}, u32[]{:S(2)}) collective-permute-start(bf16[16,1536]{1,0:T(8,128)(2,1)S(1)} %slice.262), channel_id=1, source_target_pairs={{0,16},{1,17},{2,18},{3,19},{4,20},{5,21},{6,22},{7,23},{8,24},{9,... | collective-permute-start | bytes 147464 | tf_op jit(solution)/shard_map/ppermute | solution.py:601
  397.0 9.9 %copy-start.6 = (f32[21600]{0:T(1024)S(1)}, f32[21600]{0:T(1024)}, u32[]{:S(2)}) copy-start(f32[21600]{0:T(1024)} %param.31) | copy-start | bytes 259204
  397.1 9.9 %copy-start.16 = (f32[21600]{0:T(1024)S(1)}, f32[21600]{0:T(1024)}, u32[]{:S(2)}) copy-start(f32[21600]{0:T(1024)} %param.32) | copy-start | bytes 259204
  397.1 9.9 %copy-start.17 = (f32[21600]{0:T(1024)S(1)}, f32[21600]{0:T(1024)}, u32[]{:S(2)}) copy-start(f32[21600]{0:T(1024)} %param.33) | copy-start | bytes 259204
  397.1 7.2 %collective-permute-start.18 = (bf16[32,4480]{1,0:T(8,128)(2,1)S(1)}, bf16[32,4480]{1,0:T(8,128)(2,1)S(1)}, u32[]{:S(2)}, u32[]{:S(2)}) collective-permute-start(bf16[32,4480]{1,0:T(8,128)(2,1)S(1)} %slice.258), channel_id=1, source_target_pairs={{0,8},{1,9},{2,10},{3,11},{4,12},{5,13},{6,14},{7,15},{8,0},{9,1},... | collective-permute-start | bytes 860168 | tf_op jit(solution)/shard_map/ppermute | solution.py:601
  398.0 14.3 %copy-start.7 = (f32[21600]{0:T(1024)}, f32[21600]{0:T(1024)S(1)}, u32[]{:S(2)}) copy-start(f32[21600]{0:T(1024)S(1)} %reshape_reshape.18) | copy-start | bytes 259204
  398.0 14.5 %copy-start.8 = (f32[7200]{0:T(1024)S(1)}, f32[7200]{0:T(1024)}, u32[]{:S(2)}) copy-start(f32[7200]{0:T(1024)} %param.34) | copy-start | bytes 86404
  398.0 14.5 %copy-start.19 = (f32[7200]{0:T(1024)S(1)}, f32[7200]{0:T(1024)}, u32[]{:S(2)}) copy-start(f32[7200]{0:T(1024)} %param.35) | copy-start | bytes 86404
  398.1 14.5 %copy-start.20 = (f32[7200]{0:T(1024)S(1)}, f32[7200]{0:T(1024)}, u32[]{:S(2)}) copy-start(f32[7200]{0:T(1024)} %param.36) | copy-start | bytes 86404
  398.1 15.2 %copy-start.2 = (f32[28800]{0:T(1024)S(1)}, f32[28800]{0:T(1024)}, u32[]{:S(2)}) copy-start(f32[28800]{0:T(1024)} %param.40) | copy-start | bytes 345604
  398.1 15.2 %copy-start.10 = (f32[28800]{0:T(1024)S(1)}, f32[28800]{0:T(1024)}, u32[]{:S(2)}) copy-start(f32[28800]{0:T(1024)} %param.41) | copy-start | bytes 345604
  398.1 15.2 %copy-start.11 = (f32[28800]{0:T(1024)S(1)}, f32[28800]{0:T(1024)}, u32[]{:S(2)}) copy-start(f32[28800]{0:T(1024)} %param.42) | copy-start | bytes 345604
  404.4 9.6 %copy-start.3 = (f32[28800]{0:T(1024)S(1)}, f32[28800]{0:T(1024)}, u32[]{:S(2)}) copy-start(f32[28800]{0:T(1024)} %param.37) | copy-start | bytes 345604
  404.4 9.6 %copy-start.12 = (f32[28800]{0:T(1024)S(1)}, f32[28800]{0:T(1024)}, u32[]{:S(2)}) copy-start(f32[28800]{0:T(1024)} %param.38) | copy-start | bytes 345604
  404.4 9.6 %copy-start.13 = (f32[28800]{0:T(1024)S(1)}, f32[28800]{0:T(1024)}, u32[]{:S(2)}) copy-start(f32[28800]{0:T(1024)} %param.39) | copy-start | bytes 345604
  404.5 7.6 %collective-permute-start.19 = (bf16[16,4480]{1,0:T(8,128)(2,1)S(1)}, bf16[16,4480]{1,0:T(8,128)(2,1)S(1)}, u32[]{:S(2)}, u32[]{:S(2)}) collective-permute-start(bf16[16,4480]{1,0:T(8,128)(2,1)S(1)} %slice.260), channel_id=1, source_target_pairs={{0,16},{1,17},{2,18},{3,19},{4,20},{5,21},{6,22},{7,23},{8,24},{9,... | collective-permute-start | bytes 430088 | tf_op jit(solution)/shard_map/ppermute | solution.py:601
  412.2 2.6 copy-start.9
  (3 other events, 6.9 us)
